TPU v7x, 32 devices: a whole 2x2x4 slice. The times are simulated.
32 devices in a mesh: fsdp: 8 (over z, x), expert: 4 (over y, core).
Axes of the slice: x: 2, y: 2, z: 4, core: 2. Of those that a mesh axis runs over, the one named last changes fastest.
Arguments:
- inputs: bfloat16 [2, 32, 197, 512], P(None, ('fsdp', 'expert')), may hold values from -6 to 6
- gain_attn: bfloat16 [512], P('fsdp'), may hold values from 0.5 to 1.5
- qkv_weight: bfloat16 [512, 1536], P('fsdp'), may hold values from -0.25 to 0.25
- out_weight: bfloat16 [512, 512], P('fsdp'), may hold values from -2 to 2
- gain_moe: bfloat16 [512], P('fsdp'), may hold values from 0.5 to 1.5
- router_weight: bfloat16 [512, 8], P('fsdp'), may hold values from -0.1875 to 0.1875
- expert_in: bfloat16 [8, 512, 2048], P('expert', 'fsdp'), may hold values from -0.25 to 0.25
- expert_out: bfloat16 [8, 2048, 512], P('expert', 'fsdp'), may hold values from -2 to 2
- routes: int32 [2, 32, 197, 2], P(None, ('fsdp', 'expert')), may hold values from 0 to 7, all different within a row; in each aligned block of 197 rows (0 to 196, 197 to 393, ..., all dimensions but the last counted through in order) at most 62 rows name the same one
- cotangent: bfloat16 [2, 32, 197, 512], P(None, ('fsdp', 'expert')), may hold values from -6 to 6
Outputs:
- activations: bfloat16 [2, 32, 197, 512], P(None, ('fsdp', 'expert'))
- input_grad: float32 [2, 32, 197, 512], P(None, ('fsdp', 'expert'))
- grad_gain_attn: float32 [512], P('fsdp')
- grad_qkv: float32 [512, 1536], P('fsdp')
- grad_out: float32 [512, 512], P('fsdp')
- grad_gain_moe: float32 [512], P('fsdp')
- grad_router: float32 [512, 8], P('fsdp')
- grad_expert_in: float32 [8, 512, 2048], P('expert', 'fsdp')
- grad_expert_out: float32 [8, 2048, 512], P('expert', 'fsdp')
Inputs may be any that keep to these rules, and one draw needn't show every extreme that they name: `routes`: each token names two different experts; among the 197 tokens of one device in one micro-batch no expert is named more than 62 times, a bound that some block reaches.
All inputs are finite; a program needn't handle non-finite values.
Results may differ from a plain program's by a relative error of at most 0.023.
Values may be sent and summed in bfloat16 or wider, within the bound.
A program may use at most 128 MiB of HBM per device.

v0:
```python
from functools import partial
import math

import jax
import jax.numpy as jnp
from jax import lax
from jax.sharding import PartitionSpec as P

HEADS = 8


EPS = 1e-06


def layer_norm(values, gain):
    center = jnp.mean(values, axis=-1, keepdims=True)
    shifted = values - center
    spread = jnp.mean(shifted * shifted, axis=-1, keepdims=True)
    return shifted * lax.rsqrt(spread + EPS) * gain


def slot_table(routed, count):
    order = jnp.transpose(routed).reshape(-1)
    onehot = (order[:, None] == jnp.arange(count, dtype=jnp.int32)[None, :]).astype(jnp.int32)
    ranks = jnp.cumsum(onehot, axis=0) - 1
    placed = jnp.sum(onehot * ranks, axis=1)
    return jnp.transpose(placed.reshape(2, -1))


def body(
    inputs,
    gain_attn,
    qkv_weight,
    out_weight,
    gain_moe,
    router_weight,
    expert_in,
    expert_out,
    routes,
    cotangent,
):
    micro, images, seq, width = inputs.shape
    rows = images * seq
    peers = lax.axis_size("expert")
    experts = expert_in.shape[0] * peers
    capacity = max(2, 10 * rows // (4 * experts) + 1)
    heads = HEADS
    head_width = width // heads
    scale = 1.0 / math.sqrt(head_width)
    softmax_last = partial(jax.nn.softmax, axis=-1)
    totals = None
    results = []
    token_grads = []
    for batch in range(micro):
        fetched = (
            lax.all_gather(gain_attn, "fsdp", axis=0, tiled=True),
            lax.all_gather(qkv_weight, "fsdp", axis=0, tiled=True),
            lax.all_gather(out_weight, "fsdp", axis=0, tiled=True),
            lax.all_gather(gain_moe, "fsdp", axis=0, tiled=True),
            lax.all_gather(router_weight, "fsdp", axis=0, tiled=True),
            lax.all_gather(expert_in, "fsdp", axis=1, tiled=True),
            lax.all_gather(expert_out, "fsdp", axis=1, tiled=True),
        )
        gain_one, qkv_w, out_w, gain_two, router_w, first_w, second_w = fetched
        tokens = inputs[batch].reshape(rows, width).astype(jnp.float32)
        routed = routes[batch].reshape(rows, 2)
        places = routed * capacity + slot_table(routed, experts)
        flat_places = places.reshape(-1)
        normed, pull_one = jax.vjp(layer_norm, tokens, gain_one.astype(jnp.float32))
        normed_low = normed.astype(jnp.bfloat16)
        joined = jnp.dot(normed_low, qkv_w, preferred_element_type=jnp.float32).astype(jnp.bfloat16)
        split = joined.reshape(images, seq, 3, heads, head_width)
        query, keys, values = (split[:, :, 0], split[:, :, 1], split[:, :, 2])
        scores = (
            jnp.einsum("bqhd,bkhd->bhqk", query, keys, preferred_element_type=jnp.float32) * scale
        )
        highest = jnp.max(scores, axis=-1, keepdims=True)
        log_total = highest + jnp.log(jnp.sum(jnp.exp(scores - highest), axis=-1, keepdims=True))
        probs_low = jnp.exp(scores - log_total).astype(jnp.bfloat16)
        attended = jnp.einsum(
            "bhqk,bkhd->bqhd", probs_low, values, preferred_element_type=jnp.float32
        )
        attended = attended.reshape(rows, width).astype(jnp.bfloat16)
        middle = tokens + jnp.dot(attended, out_w, preferred_element_type=jnp.float32)
        normed_two, pull_two = jax.vjp(layer_norm, middle, gain_two.astype(jnp.float32))
        normed_two_low = normed_two.astype(jnp.bfloat16)
        logits = jnp.dot(normed_two_low, router_w, preferred_element_type=jnp.float32)
        gates, pull_gates = jax.vjp(softmax_last, logits)
        chosen = jnp.take_along_axis(gates, routed, axis=1)
        outgoing = (
            jnp.zeros((experts * capacity, width), jnp.bfloat16)
            .at[flat_places]
            .set(jnp.repeat(normed_two_low, 2, axis=0))
            .reshape(experts, capacity, width)
        )
        arrived = lax.all_to_all(outgoing, "expert", split_axis=0, concat_axis=1, tiled=True)
        hidden = jnp.einsum("ecd,edf->ecf", arrived, first_w, preferred_element_type=jnp.float32)
        acted, pull_acted = jax.vjp(jax.nn.gelu, hidden)
        acted_low = acted.astype(jnp.bfloat16)
        produced = jnp.einsum(
            "ecf,efd->ecd", acted_low, second_w, preferred_element_type=jnp.float32
        ).astype(jnp.bfloat16)
        returned = lax.all_to_all(produced, "expert", split_axis=1, concat_axis=0, tiled=True)
        picked = returned.reshape(experts * capacity, width)[places].astype(jnp.float32)
        outputs = middle + jnp.sum(chosen[..., None] * picked, axis=1)
        results.append(outputs.astype(jnp.bfloat16))
        fetched = (
            lax.all_gather(gain_attn, "fsdp", axis=0, tiled=True),
            lax.all_gather(qkv_weight, "fsdp", axis=0, tiled=True),
            lax.all_gather(out_weight, "fsdp", axis=0, tiled=True),
            lax.all_gather(gain_moe, "fsdp", axis=0, tiled=True),
            lax.all_gather(router_weight, "fsdp", axis=0, tiled=True),
            lax.all_gather(expert_in, "fsdp", axis=1, tiled=True),
            lax.all_gather(expert_out, "fsdp", axis=1, tiled=True),
        )
        gain_one, qkv_w, out_w, gain_two, router_w, first_w, second_w = fetched
        upstream = cotangent[batch].reshape(rows, width).astype(jnp.float32)
        grad_picked = upstream[:, None, :] * chosen[..., None]
        grad_chosen = jnp.sum(upstream[:, None, :] * picked, axis=-1)
        grad_outgoing = (
            jnp.zeros((experts * capacity, width), jnp.bfloat16)
            .at[flat_places]
            .set(grad_picked.reshape(-1, width).astype(jnp.bfloat16))
            .reshape(experts, capacity, width)
        )
        grad_arrived = lax.all_to_all(
            grad_outgoing, "expert", split_axis=0, concat_axis=1, tiled=True
        )
        grad_acted = jnp.einsum(
            "ecd,efd->ecf", grad_arrived, second_w, preferred_element_type=jnp.float32
        )
        part_second = jnp.einsum(
            "ecf,ecd->efd", acted_low, grad_arrived, preferred_element_type=jnp.float32
        )
        grad_hidden = pull_acted(grad_acted)[0].astype(jnp.bfloat16)
        part_first = jnp.einsum(
            "ecd,ecf->edf", arrived, grad_hidden, preferred_element_type=jnp.float32
        )
        grad_sent = jnp.einsum(
            "ecf,edf->ecd", grad_hidden, first_w, preferred_element_type=jnp.float32
        ).astype(jnp.bfloat16)
        grad_returned = lax.all_to_all(grad_sent, "expert", split_axis=1, concat_axis=0, tiled=True)
        grad_normed_two = jnp.sum(
            grad_returned.reshape(experts * capacity, width)[places].astype(jnp.float32), axis=1
        )
        onehot = (routed[..., None] == jnp.arange(experts, dtype=jnp.int32)).astype(jnp.float32)
        grad_gates = jnp.sum(onehot * grad_chosen[..., None], axis=1)
        grad_logits = pull_gates(grad_gates)[0].astype(jnp.bfloat16)
        part_router = jnp.dot(normed_two_low.T, grad_logits, preferred_element_type=jnp.float32)
        grad_normed_two = grad_normed_two + jnp.dot(
            grad_logits, router_w.T, preferred_element_type=jnp.float32
        )
        grad_middle_norm, part_gain_two = pull_two(grad_normed_two)
        grad_middle = upstream + grad_middle_norm
        grad_branch = grad_middle.astype(jnp.bfloat16)
        part_out = jnp.dot(attended.T, grad_branch, preferred_element_type=jnp.float32)
        grad_attended = jnp.dot(grad_branch, out_w.T, preferred_element_type=jnp.float32).astype(
            jnp.bfloat16
        )
        grad_attended = grad_attended.reshape(images, seq, heads, head_width)
        scores = (
            jnp.einsum("bqhd,bkhd->bhqk", query, keys, preferred_element_type=jnp.float32) * scale
        )
        probs = jnp.exp(scores - log_total)
        probs_low = probs.astype(jnp.bfloat16)
        grad_probs = jnp.einsum(
            "bqhd,bkhd->bhqk", grad_attended, values, preferred_element_type=jnp.float32
        )
        grad_values = jnp.einsum(
            "bhqk,bqhd->bkhd", probs_low, grad_attended, preferred_element_type=jnp.float32
        )
        grad_scores = probs * (grad_probs - jnp.sum(grad_probs * probs, axis=-1, keepdims=True))
        grad_scores = grad_scores.astype(jnp.bfloat16)
        grad_query = (
            jnp.einsum("bhqk,bkhd->bqhd", grad_scores, keys, preferred_element_type=jnp.float32)
            * scale
        )
        grad_keys = (
            jnp.einsum("bhqk,bqhd->bkhd", grad_scores, query, preferred_element_type=jnp.float32)
            * scale
        )
        grad_joined = (
            jnp.stack([grad_query, grad_keys, grad_values], axis=2)
            .reshape(rows, 3 * width)
            .astype(jnp.bfloat16)
        )
        part_qkv = jnp.dot(normed_low.T, grad_joined, preferred_element_type=jnp.float32)
        grad_normed = jnp.dot(grad_joined, qkv_w.T, preferred_element_type=jnp.float32)
        grad_tokens_norm, part_gain_one = pull_one(grad_normed)
        token_grads.append(grad_middle + grad_tokens_norm)
        parts = (
            part_gain_one,
            part_qkv,
            part_out,
            part_gain_two,
            part_router,
            part_first,
            part_second,
        )
        totals = parts if totals is None else tuple((a + b for a, b in zip(totals, parts)))
    summed = (
        lax.psum_scatter(
            totals[0].astype(jnp.bfloat16), "fsdp", scatter_dimension=0, tiled=True
        ).astype(jnp.float32),
        lax.psum_scatter(
            totals[1].astype(jnp.bfloat16), "fsdp", scatter_dimension=0, tiled=True
        ).astype(jnp.float32),
        lax.psum_scatter(
            totals[2].astype(jnp.bfloat16), "fsdp", scatter_dimension=0, tiled=True
        ).astype(jnp.float32),
        lax.psum_scatter(
            totals[3].astype(jnp.bfloat16), "fsdp", scatter_dimension=0, tiled=True
        ).astype(jnp.float32),
        lax.psum_scatter(
            totals[4].astype(jnp.bfloat16), "fsdp", scatter_dimension=0, tiled=True
        ).astype(jnp.float32),
        lax.psum_scatter(
            totals[5].astype(jnp.bfloat16), "fsdp", scatter_dimension=1, tiled=True
        ).astype(jnp.float32),
        lax.psum_scatter(
            totals[6].astype(jnp.bfloat16), "fsdp", scatter_dimension=1, tiled=True
        ).astype(jnp.float32),
    )
    dense = (
        lax.psum(summed[0].astype(jnp.bfloat16), "expert").astype(jnp.float32),
        lax.psum(summed[1].astype(jnp.bfloat16), "expert").astype(jnp.float32),
        lax.psum(summed[2].astype(jnp.bfloat16), "expert").astype(jnp.float32),
        lax.psum(summed[3].astype(jnp.bfloat16), "expert").astype(jnp.float32),
        lax.psum(summed[4].astype(jnp.bfloat16), "expert").astype(jnp.float32),
    )
    activations = jnp.stack(results).reshape(inputs.shape)
    input_grad = jnp.stack(token_grads).reshape(inputs.shape)
    return (
        activations,
        input_grad,
        dense[0],
        dense[1],
        dense[2],
        dense[3],
        dense[4],
        summed[5],
        summed[6],
    )


def solution(mesh):
    return jax.shard_map(
        body,
        mesh=mesh,
        in_specs=(
            P(None, ("fsdp", "expert"), None, None),
            P("fsdp"),
            P("fsdp", None),
            P("fsdp", None),
            P("fsdp"),
            P("fsdp", None),
            P("expert", "fsdp", None),
            P("expert", "fsdp", None),
            P(None, ("fsdp", "expert"), None, None),
            P(None, ("fsdp", "expert"), None, None),
        ),
        out_specs=(
            P(None, ("fsdp", "expert"), None, None),
            P(None, ("fsdp", "expert"), None, None),
            P("fsdp"),
            P("fsdp", None),
            P("fsdp", None),
            P("fsdp"),
            P("fsdp", None),
            P("expert", "fsdp", None),
            P("expert", "fsdp", None),
        ),
        check_vma=False,
    )
```

profile of v0, /device:TPU:0, one launch (start us, length us, event | category | flops | bytes accessed | tf_op | source)
XLA Modules:
  0.0 816.1 jit_solution(7326933539415086252)
XLA Ops:
  15.1 23.2 %all-reduce.7 = (bf16[512]{0:T(512)(128)(2,1)S(1)}, bf16[512]{0:T(512)(128)(2,1)S(1)}) all-reduce(bf16[512]{0:T(512)(128)(2,1)S(1)} %dynamic-update-slice, bf16[512]{0:T(512)(128)(2,1)S(1)} %dynamic-update-slice.1), channel_id=1, replica_groups=mesh['fsdp'=8,'expert'=4] {'fsdp'}, use_global_device_ids=true, to_apply=%add.2 | all-reduce | flops 1024 | bytes 4096
  49.3 26.1 %all-gather = bf16[8,64,8]{1,2,0:T(8,128)(2,1)S(1)} all-gather(bf16[1,64,8]{1,2,0:T(8,128)(2,1)S(1)} %bitcast.370), channel_id=1, replica_groups=mesh['fsdp'=8,'expert'=4] {'fsdp'}, dimensions={0}, use_global_device_ids=true | all-gather | bytes 9216 | tf_op jit(solution)/shard_map/all_gather | solution.py:60
  79.0 32.7 %all_gather.16 = bf16[512,512]{1,0:T(8,128)(2,1)S(1)} all-gather(bf16[64,512]{1,0:T(8,128)(2,1)S(1)} %copy-done.44), channel_id=1, replica_groups=mesh['fsdp'=8,'expert'=4] {'fsdp'}, dimensions={0}, use_global_device_ids=true | all-gather | bytes 589824 | tf_op jit(solution)/shard_map/all_gather | solution.py:58
  123.5 4.6 gather_fusion.4
  128.5 3.0 scatter_custom_fusion.2
  132.4 4.1 all-to-all-start.4
  142.1 3.3 scatter_custom_fusion
  149.5 4.1 all-to-all-start
  166.4 5.6 fusion.122
  172.0 38.6 %all-gather.7.cloned.1.call-done = bf16[2,512,2048]{2,1,0:T(8,128)(2,1)} async-done(((bf16[2,64,2048]{2,1,0:T(8,128)(2,1)}), bf16[2,512,2048]{2,1,0:T(8,128)(2,1)}) %all-gather.7.cloned.1.call-update) | async-done | bytes 4194320 | tf_op jit(solution)/shard_map/all_gather | solution.py:61
  210.6 9.0 %fusion.6 = (bf16[2,248,2048]{2,1,0:T(8,128)(2,1)S(1)}, f32[2,248,2048]{2,1,0:T(8,128)}) fusion(f32[2,248,2048]{2,1,0:T(8,128)} %fusion.122, bf16[2,248,512]{2,1,0:T(8,128)(2,1)} %all_to_all.99, bf16[2,512,2048]{2,1,0:T(8,128)(2,1)} %all-gather.7.cloned.1.call-done), kind=kOutput, calls=%fused_computation.22 | convolution fusion | flops 1060503552 | bytes 14860288 | tf_op jit(solution)/shard_map/ecd,edf->ecf/dot_general | solution.py:97
  223.4 4.1 all-to-all-start.5
  227.6 4.9 convolution_convert_fusion.5
  233.7 2.6 all-to-all-done.5
  236.3 4.5 all-to-all-start.1
  246.5 3.7 gather_fusion.2
  256.5 3.7 gather_fusion
  262.6 3.5 multiply_reduce_fusion.3
  269.8 2.9 reduce_sum.359
  284.5 3.2 multiply_reduce_fusion.1
  289.1 4.6 gather_fusion.5
  297.1 3.4 scatter_custom_fusion.3
  302.5 4.3 all-to-all-start.6
  310.6 3.2 scatter_custom_fusion.1
  321.0 3.5 all-to-all-start.2
  326.8 2.5 fusion.92
  330.6 2.7 all-to-all-done.2
  333.5 3.7 fusion.123
  337.2 4.8 fusion.13
  345.7 3.5 all-to-all-start.7
  349.2 4.9 convolution_convert_fusion.4
  357.8 4.1 all-to-all-start.3
  375.6 2.6 gather_fusion.1
  380.7 3.4 multiply_reduce_fusion.2
  392.8 2.7 multiply_reduce_fusion
  395.4 2.6 fusion.15
  407.4 6.3 fusion.125
  413.6 45.3 %reduce-scatter.10.cloned.1.call-done = bf16[64,512]{1,0:T(8,128)(2,1)} async-done(((bf16[512,512]{1,0:T(8,128)(2,1)}), bf16[64,512]{1,0:T(8,128)(2,1)}) %reduce-scatter.10.cloned.1.call-update) | async-done | bytes 65552 | tf_op jit(solution)/shard_map/reduce_scatter | solution.py:208
  458.9 67.6 %reduce-scatter.8.cloned.1.call-done = bf16[64,1536]{1,0:T(8,128)(2,1)} async-done(((bf16[512,1536]{1,0:T(8,128)(2,1)}), bf16[64,1536]{1,0:T(8,128)(2,1)}) %reduce-scatter.8.cloned.1.call-update) | async-done | bytes 196624 | tf_op jit(solution)/shard_map/reduce_scatter | solution.py:205
  526.9 6.7 add_convert_fusion.1
  534.6 3.8 fusion.109
  538.4 3.6 add_convert_fusion
  551.3 19.3 %all-reduce.6 = (bf16[512]{0:T(512)(128)(2,1)S(1)}, bf16[512]{0:T(512)(128)(2,1)S(1)}) all-reduce(bf16[512]{0:T(512)(128)(2,1)S(1)} %add_convert_fusion.5, bf16[512]{0:T(512)(128)(2,1)S(1)} %add_convert_fusion.4), channel_id=2, replica_groups=mesh['fsdp'=8,'expert'=4] {'fsdp'}, use_global_device_ids=true, to_apply=%region_48.50.clone | all-reduce | flops 1024 | bytes 4096
  570.8 19.3 %reduce-scatter.16.cloned.1.call-done = bf16[64,8]{1,0:T(8,128)(2,1)} async-done(((bf16[512,8]{1,0:T(8,128)(2,1)}), bf16[64,8]{1,0:T(8,128)(2,1)}) %reduce-scatter.16.cloned.1.call-update) | async-done | bytes 1040
  590.9 5.6 all-reduce.8
  598.1 25.5 %all-reduce.12.cloned.1.call-done = (bf16[64,1536]{1,0:T(8,128)(2,1)}, bf16[64,512]{1,0:T(8,128)(2,1)}) async-done(((bf16[64,1536]{1,0:T(8,128)(2,1)}, bf16[64,512]{1,0:T(8,128)(2,1)}), (bf16[64,1536]{1,0:T(8,128)(2,1)}, bf16[64,512]{1,0:T(8,128)(2,1)})) %all-reduce.12.cloned.1.call-update) | async-done | bytes 262160 | tf_op jit(solution)/shard_map/psum | solution.py:226
  626.9 88.8 %reduce-scatter.12.cloned.1.call-done = bf16[2,64,2048]{2,1,0:T(8,128)(2,1)} async-done(((bf16[2,512,2048]{2,1,0:T(8,128)(2,1)}), bf16[2,64,2048]{2,1,0:T(8,128)(2,1)}) %reduce-scatter.12.cloned.1.call-update) | async-done | bytes 524304 | tf_op jit(solution)/shard_map/reduce_scatter | solution.py:217
  717.8 89.2 %reduce-scatter.14.cloned.1.call-done = bf16[2,256,512]{2,1,0:T(8,128)(2,1)} async-done(((bf16[2,2048,512]{2,1,0:T(8,128)(2,1)}), bf16[2,256,512]{2,1,0:T(8,128)(2,1)}) %reduce-scatter.14.cloned.1.call-update) | async-done | bytes 524304 | tf_op jit(solution)/shard_map/reduce_scatter | solution.py:220
  (374 shorter events, 173.7 us)
Async XLA Ops:
  7.2 34.1 %copy-start.41 = (bf16[2,1,197,512]{3,0,2,1:T(2,128)(2,1)S(1)}, bf16[2,1,197,512]{3,0,2,1:T(2,128)(2,1)}, u32[]{:S(2)}) copy-start(bf16[2,1,197,512]{3,0,2,1:T(2,128)(2,1)} %param.21) | copy-start | bytes 1210372
  7.2 104.6 %all-gather.5.cloned.1.call-start = ((), (), s32[]{:S(2)}) async-start(), calls=%async_computation.13 | async-start | bytes 1769472 | tf_op jit(solution)/shard_map/all_gather | solution.py:57
  7.9 158.5 %all-gather.9.cloned.1.call-start = ((), (), s32[]{:S(2)}) async-start(), calls=%async_computation.15 | async-start | bytes 4718592 | tf_op jit(solution)/shard_map/all_gather | solution.py:62
  8.7 201.9 %all-gather.7.cloned.1.call-start = ((), (), s32[]{:S(2)}) async-start(), calls=%async_computation.14 | async-start | bytes 4718592 | tf_op jit(solution)/shard_map/all_gather | solution.py:61
  39.2 37.6 %copy-start.26 = (s32[1,1,197,2]{3,2,1,0:T(8,128)}, s32[1,1,197,2]{3,2,1,0:T(8,128)S(1)}, u32[]{:S(2)}) copy-start(s32[1,1,197,2]{3,2,1,0:T(8,128)S(1)} %copy.263) | copy-start | bytes 4732
  42.8 32.6 %copy-start.25 = (f32[197,512]{1,0:T(8,128)}, f32[197,512]{1,0:T(8,128)S(1)}, u32[]{:S(2)}) copy-start(f32[197,512]{1,0:T(8,128)S(1)} %get-tuple-element.138) | copy-start | bytes 1210372
  43.8 35.2 %copy-start.44 = (bf16[64,512]{1,0:T(8,128)(2,1)S(1)}, bf16[64,512]{1,0:T(8,128)(2,1)}, u32[]{:S(2)}) copy-start(bf16[64,512]{1,0:T(8,128)(2,1)} %param.15) | copy-start | bytes 196612
  77.6 43.8 %copy-start.6 = (bf16[1,1,197,512]{3,2,1,0:T(8,128)(2,1)}, bf16[1,1,197,512]{3,2,1,0:T(8,128)(2,1)S(1)}, u32[]{:S(2)}) copy-start(bf16[1,1,197,512]{3,2,1,0:T(8,128)(2,1)S(1)} %get-tuple-element.136) | copy-start | bytes 605188
  78.4 39.8 %copy-start.66 = (f32[197]{0:T(256)}, f32[197]{0:T(256)S(1)}, u32[]{:S(2)}) copy-start(f32[197]{0:T(256)S(1)} %fusion.43) | copy-start | bytes 2368
  78.4 39.8 %copy-start.49 = (f32[197]{0:T(256)}, f32[197]{0:T(256)S(1)}, u32[]{:S(2)}) copy-start(f32[197]{0:T(256)S(1)} %fusion.105) | copy-start | bytes 2368
  78.4 39.8 %copy-start.58 = (f32[197]{0:T(256)}, f32[197]{0:T(256)S(1)}, u32[]{:S(2)}) copy-start(f32[197]{0:T(256)S(1)} %fusion.103) | copy-start | bytes 2368
  79.0 49.5 %copy-start.72 = (s32[394,1]{0,1:T(1,128)}, s32[394,1]{0,1:T(1,128)S(1)}, u32[]{:S(2)}) copy-start(s32[394,1]{0,1:T(1,128)S(1)} %compare_select_fusion.5) | copy-start | bytes 4732
  111.7 9.6 %copy-start.1 = (bf16[512,512]{1,0:T(8,128)(2,1)}, bf16[512,512]{1,0:T(8,128)(2,1)S(1)}, u32[]{:S(2)}) copy-start(bf16[512,512]{1,0:T(8,128)(2,1)S(1)} %all_gather.16) | copy-start | bytes 1572868
  123.4 145.0 %copy-start.53 = (f32[197]{0:T(256)}, f32[197]{0:T(256)S(1)}, u32[]{:S(2)}) copy-start(f32[197]{0:T(256)S(1)} %get-tuple-element.114) | copy-start | bytes 2368
  123.5 30.1 %copy-start.63 = (f32[197]{0:T(256)}, f32[197]{0:T(256)S(1)}, u32[]{:S(2)}) copy-start(f32[197]{0:T(256)S(1)} %fusion.100) | copy-start | bytes 2368
  128.3 8.2 %copy-start.43 = (f32[197,2]{1,0:T(8,128)}, f32[197,2]{1,0:T(8,128)S(1)}, u32[]{:S(2)}) copy-start(f32[197,2]{1,0:T(8,128)S(1)} %and_select_fusion.1) | copy-start | bytes 4732
  132.4 17.0 %all-to-all-start.4 = ((bf16[8,62,512]{2,1,0:T(8,128)(2,1)}), bf16[8,62,512]{2,1,0:T(8,128)(2,1)}, u32[]{:S(2)}, u32[]{:S(2)}) async-start(bf16[8,62,512]{2,1,0:T(8,128)(2,1)} %reshape.647), calls=%async_computation.4 | async-start | bytes 1048576 | tf_op jit(solution)/shard_map/all_to_all | solution.py:126
  149.5 13.1 %all-to-all-start = ((bf16[8,62,512]{2,1,0:T(8,128)(2,1)}), bf16[8,62,512]{2,1,0:T(8,128)(2,1)}, u32[]{:S(2)}, u32[]{:S(2)}) async-start(bf16[8,62,512]{2,1,0:T(8,128)(2,1)} %reshape.633), calls=%async_computation | async-start | bytes 1048576 | tf_op jit(solution)/shard_map/all_to_all | solution.py:96
  210.6 10.3 %copy-start.73 = (bf16[2,512,2048]{2,1,0:T(8,128)(2,1)S(1)}, bf16[2,512,2048]{2,1,0:T(8,128)(2,1)}, u32[]{:S(2)}) copy-start(bf16[2,512,2048]{2,1,0:T(8,128)(2,1)} %all-gather.7.cloned.1.call-done) | copy-start | bytes 12582916
  223.4 12.9 %all-to-all-start.5 = ((bf16[2,248,512]{2,0,1:T(2,128)(2,1)}), bf16[2,248,512]{2,0,1:T(2,128)(2,1)}, u32[]{:S(2)}, u32[]{:S(2)}) async-start(bf16[2,248,512]{2,0,1:T(2,128)(2,1)} %copy.220), calls=%async_computation.5 | async-start | bytes 1015808 | tf_op jit(solution)/shard_map/all_to_all | solution.py:142
  236.3 16.3 %all-to-all-start.1 = ((bf16[2,248,512]{2,0,1:T(2,128)(2,1)}), bf16[2,248,512]{2,0,1:T(2,128)(2,1)}, u32[]{:S(2)}, u32[]{:S(2)}) async-start(bf16[2,248,512]{2,0,1:T(2,128)(2,1)} %copy.205), calls=%async_computation.1 | async-start | bytes 1015808 | tf_op jit(solution)/shard_map/all_to_all | solution.py:103
  240.8 34.6 %copy-start.46 = (f32[197]{0:T(256)}, f32[197]{0:T(256)S(1)}, u32[]{:S(2)}) copy-start(f32[197]{0:T(256)S(1)} %broadcast_multiply_fusion) | copy-start | bytes 2368
  242.1 14.4 %copy-start.68 = (f32[197]{0:T(256)}, f32[197]{0:T(256)S(1)}, u32[]{:S(2)}) copy-start(f32[197]{0:T(256)S(1)} %multiply_reduce_fusion.10) | copy-start | bytes 2368
  277.8 10.0 %copy-start.54 = (f32[197]{0:T(256)}, f32[197]{0:T(256)S(1)}, u32[]{:S(2)}) copy-start(f32[197]{0:T(256)S(1)} %negate_multiply_fusion.3) | copy-start | bytes 2368
  293.7 22.1 %copy-start.45 = (f32[8,197]{1,0:T(8,128)S(1)}, f32[8,197]{1,0:T(8,128)}, u32[]{:S(2)}) copy-start(f32[8,197]{1,0:T(8,128)} %get-tuple-element.130) | copy-start | bytes 18916
  302.5 18.4 %all-to-all-start.6 = ((bf16[8,62,512]{2,1,0:T(8,128)(2,1)}), bf16[8,62,512]{2,1,0:T(8,128)(2,1)}, u32[]{:S(2)}, u32[]{:S(2)}) async-start(bf16[8,62,512]{2,1,0:T(8,128)(2,1)} %reshape.650), calls=%async_computation.6 | async-start | bytes 1048576 | tf_op jit(solution)/shard_map/all_to_all | solution.py:126
  306.8 13.6 %copy-start.62 = (f32[197]{0:T(256)S(1)}, f32[197]{0:T(256)}, u32[]{:S(2)}) copy-start(f32[197]{0:T(256)} %copy-done.61) | copy-start | bytes 2368
  315.8 11.0 %copy-start.55 = (f32[197]{0:T(256)S(1)}, f32[197]{0:T(256)}, u32[]{:S(2)}) copy-start(f32[197]{0:T(256)} %copy-done.54) | copy-start | bytes 2368
  321.0 12.3 %all-to-all-start.2 = ((bf16[8,62,512]{2,1,0:T(8,128)(2,1)}), bf16[8,62,512]{2,1,0:T(8,128)(2,1)S(1)}, u32[]{:S(2)}, u32[]{:S(2)}) async-start(bf16[8,62,512]{2,1,0:T(8,128)(2,1)} %reshape.644), calls=%async_computation.2 | async-start | bytes 1048576 | tf_op jit(solution)/shard_map/all_to_all | solution.py:96
  345.7 12.1 %all-to-all-start.7 = ((bf16[2,248,512]{2,0,1:T(2,128)(2,1)}), bf16[2,248,512]{2,0,1:T(2,128)(2,1)S(1)}, u32[]{:S(2)}, u32[]{:S(2)}) async-start(bf16[2,248,512]{2,0,1:T(2,128)(2,1)} %copy.231), calls=%async_computation.7 | async-start | bytes 1015808 | tf_op jit(solution)/shard_map/all_to_all | solution.py:142
  349.2 14.4 %copy-start.7 = (bf16[1,1,197,512]{3,2,1,0:T(8,128)(2,1)S(1)}, bf16[1,1,197,512]{3,2,1,0:T(8,128)(2,1)}, u32[]{:S(2)}) copy-start(bf16[1,1,197,512]{3,2,1,0:T(8,128)(2,1)} %copy-done.6) | copy-start | bytes 605188
  349.2 14.4 %copy-start.59 = (f32[197]{0:T(256)S(1)}, f32[197]{0:T(256)}, u32[]{:S(2)}) copy-start(f32[197]{0:T(256)} %copy-done.58) | copy-start | bytes 2368
  357.8 14.6 %all-to-all-start.3 = ((bf16[2,248,512]{2,0,1:T(2,128)(2,1)}), bf16[2,248,512]{2,0,1:T(2,128)(2,1)}, u32[]{:S(2)}, u32[]{:S(2)}) async-start(bf16[2,248,512]{2,0,1:T(2,128)(2,1)} %copy.215), calls=%async_computation.3 | async-start | bytes 1015808 | tf_op jit(solution)/shard_map/all_to_all | solution.py:103
  362.0 97.0 %reduce-scatter.10.cloned.1.call-start = ((), (), s32[]{:S(2)}) async-start(), calls=%async_computation.17 | async-start | bytes 589824 | tf_op jit(solution)/shard_map/reduce_scatter | solution.py:208
  370.6 10.0 %copy-start.24 = (f32[197,512]{1,0:T(8,128)S(1)}, f32[197,512]{1,0:T(8,128)}, u32[]{:S(2)}) copy-start(f32[197,512]{1,0:T(8,128)} %copy-done.23) | copy-start | bytes 1210372
  370.6 10.0 %copy-start.42 = (f32[197,2]{1,0:T(8,128)S(1)}, f32[197,2]{1,0:T(8,128)}, u32[]{:S(2)}) copy-start(f32[197,2]{1,0:T(8,128)} %and_select_fusion) | copy-start | bytes 4732
  374.3 11.4 %copy-start.52 = (f32[197]{0:T(256)S(1)}, f32[197]{0:T(256)}, u32[]{:S(2)}) copy-start(f32[197]{0:T(256)} %copy-done.51) | copy-start | bytes 2368
  374.3 12.8 %copy-start.4 = (f32[197,512]{1,0:T(8,128)S(1)}, f32[197,512]{1,0:T(8,128)}, u32[]{:S(2)}) copy-start(f32[197,512]{1,0:T(8,128)} %get-tuple-element.122) | copy-start | bytes 1210372
  378.2 11.1 %copy-start.47 = (f32[197]{0:T(256)S(1)}, f32[197]{0:T(256)}, u32[]{:S(2)}) copy-start(f32[197]{0:T(256)} %copy-done.46) | copy-start | bytes 2368
  378.2 12.9 %copy-start.2 = (bf16[512,512]{1,0:T(8,128)(2,1)S(1)}, bf16[512,512]{1,0:T(8,128)(2,1)}, u32[]{:S(2)}) copy-start(bf16[512,512]{1,0:T(8,128)(2,1)} %copy-done.1) | copy-start | bytes 1572868
  391.1 7.0 copy-start.13
  398.1 128.5 %reduce-scatter.8.cloned.1.call-start = ((), (), s32[]{:S(2)}) async-start(), calls=%async_computation.16 | async-start | bytes 1769472 | tf_op jit(solution)/shard_map/reduce_scatter | solution.py:205
  406.1 184.0 %reduce-scatter.16.cloned.1.call-start = ((), (), s32[]{:S(2)}) async-start(), calls=%async_computation.20 | async-start | bytes 147456
  407.3 119.6 %copy-start.36 = (bf16[2,248,2048]{2,1,0:T(8,128)(2,1)S(1)}, bf16[2,248,2048]{2,1,0:T(8,128)(2,1)}, u32[]{:S(2)}) copy-start(bf16[2,248,2048]{2,1,0:T(8,128)(2,1)} %copy-done.35) | copy-start | bytes 6094852
  407.3 119.6 %copy-start.38 = (bf16[2,248,512]{2,1,0:T(8,128)(2,1)S(1)}, bf16[2,248,512]{2,1,0:T(8,128)(2,1)}, u32[]{:S(2)}) copy-start(bf16[2,248,512]{2,1,0:T(8,128)(2,1)} %copy-done.37) | copy-start | bytes 1523716
  407.3 216.4 %all-reduce.12.cloned.1.call-start = ((), (), s32[]{:S(2)}) async-start(), calls=%async_computation.21 | async-start | bytes 524288 | tf_op jit(solution)/shard_map/psum | solution.py:226
  526.6 189.1 %reduce-scatter.12.cloned.1.call-start = ((), (), s32[]{:S(2)}) async-start(), calls=%async_computation.18 | async-start | bytes 4718592 | tf_op jit(solution)/shard_map/reduce_scatter | solution.py:217
  533.6 273.4 %reduce-scatter.14.cloned.1.call-start = ((), (), s32[]{:S(2)}) async-start(), calls=%async_computation.19 | async-start | bytes 4718592 | tf_op jit(solution)/shard_map/reduce_scatter | solution.py:220
  (44 other events, 140.3 us)
Sparse Core Ops, SparseCore 0:
  10.2 46.8 all-gather.4
  59.3 77.1 all-gather.8
  138.6 71.9 all-gather.6
  398.2 60.7 reduce-scatter.9
  462.6 63.8 reduce-scatter.7
  530.3 59.7 reduce-scatter.15
  592.5 31.1 all-reduce.11
  627.7 87.9 reduce-scatter.11
  719.3 87.6 reduce-scatter.13
where the time goes:
time: 828 us; the launch traced here: 816 us
  waiting for transfers between devices  387 us (47%)
  local copies, waits for them, and re-layouts  115 us (14%)
  blocking collectives  107 us (13%)
  matrix products  104 us (13%)
  other arithmetic  53.3 us (6%)
  starting transfers between devices  33.2 us (4%)
  between operations  17 us (2%)
    reduce_scatter x1, waiting for transfers between devices, body(): lax.psum_scatter(totals[6].astype(jnp.bfloat16), 'fsdp', scatter_dimensio...  89.2 us
    reduce_scatter x1, waiting for transfers between devices, body(): lax.psum_scatter(totals[5].astype(jnp.bfloat16), 'fsdp', scatter_dimensio...  88.8 us
    reduce_scatter x1, waiting for transfers between devices, body(): lax.psum_scatter(totals[1].astype(jnp.bfloat16), 'fsdp', scatter_dimensio...  67.6 us
    reduce_scatter x1, waiting for transfers between devices, body(): lax.psum_scatter(totals[2].astype(jnp.bfloat16), 'fsdp', scatter_dimensio...  45.3 us
    unnamed x2, blocking collectives  42.5 us
    all_gather x1, waiting for transfers between devices, body(): lax.all_gather(expert_in, 'fsdp', axis=1, tiled=True)  38.6 us
    all_gather x1, blocking collectives, body(): lax.all_gather(out_weight, 'fsdp', axis=0, tiled=True)  32.7 us
    all_gather x1, blocking collectives, body(): lax.all_gather(router_weight, 'fsdp', axis=0, tiled=True)  26.1 us
  transfers between devices with their start and end apart: 17, of which 11 were waited for; matrix products, arithmetic and copies ran while one was open for 19% of the time, Pallas kernels for 0%

commit v1 on v0

v1 whole, which is shorter than its diff:
```python
import functools
import math

import jax
import jax.numpy as jnp
from jax import lax
from jax.experimental import pallas as pl
from jax.experimental.pallas import tpu as pltpu
from jax.sharding import PartitionSpec as P

HEADS = 8
EPS = 1e-06
MESH = pl.DeviceIdType.MESH
F32 = jnp.float32
BF16 = jnp.bfloat16


def nn(a, b):
    return lax.dot_general(a, b, (((1,), (0,)), ((), ())), preferred_element_type=F32)


def nt(a, b):
    return lax.dot_general(a, b, (((1,), (1,)), ((), ())), preferred_element_type=F32)


def tn(a, b):
    return lax.dot_general(a, b, (((0,), (0,)), ((), ())), preferred_element_type=F32)


def normalize(values):
    center = jnp.mean(values, axis=-1, keepdims=True)
    shifted = values - center
    spread = jnp.mean(shifted * shifted, axis=-1, keepdims=True)
    rstd = lax.rsqrt(spread + EPS)
    return shifted * rstd, rstd


def normalize_back(grad, hat, rstd):
    return rstd * (
        grad
        - jnp.mean(grad, axis=-1, keepdims=True)
        - hat * jnp.mean(grad * hat, axis=-1, keepdims=True)
    )


class Semaphores:
    def __init__(self):
        self.used = 0

    def take(self, count):
        start = self.used
        self.used += count
        return start


def layout(mesh_shape, micro, seq, width, ff_width):
    fsdp, peers = mesh_shape["fsdp"], mesh_shape["expert"]
    c = {}
    c["nz"] = fsdp // 2
    c["E"] = peers
    c["G"] = peers // 2
    c["NE"] = 2 * peers
    c["T"] = seq
    c["TP"] = -(-seq // 16) * 16
    c["CP"] = -(-max(2, 10 * seq // (4 * 2 * peers) + 1) // 16) * 16
    c["S"] = c["NE"] * c["CP"]
    c["D"] = width
    c["FF"] = ff_width
    c["RF"] = width // fsdp
    c["CF"] = ff_width // fsdp
    c["TW"] = 4 * width // peers
    c["M"] = micro
    return c


def scratch_of(c):
    nz, E, G, NE, TP, CP, S, D, FF, RF, CF, TW, M = (
        c[k] for k in ("nz", "E", "G", "NE", "TP", "CP", "S", "D", "FF", "RF", "CF", "TW", "M")
    )
    h = nz // 2
    v = {
        "XP": ((M, TP, D), BF16),
        "CT": ((M, TP, D), BF16),
        "RT": ((M, TP, 128), jnp.int32),
        "DW": ((E, nz, 2, RF, TW), BF16),
        "SM": ((nz, 2, RF, 128), BF16),
        "WIN": ((nz, 2, RF, FF), BF16),
        "WOUT": ((nz, 2, CF, D), BF16),
        "N1": ((M, TP, D), BF16),
        "J": ((M, TP, 3 * D), BF16),
        "ATT": ((M, TP, D), BF16),
        "MID": ((M, TP, D), F32),
        "N2": ((M, TP, D), BF16),
        "GATES": ((M, TP, 128), F32),
        "PM": ((M, 2, TP, S), BF16),
        "XGS": ((M, 2, NE, CP, D), BF16),
        "XG": ((M, 2, NE, CP, D), BF16),
        "YD": ((M, 2, NE, CP, D), BF16),
        "RET": ((M, 2, NE, CP, D), BF16),
        "YACC": ((M, S, D), F32),
        "DXACC": ((M, S, D), F32),
        "AS": ((M, S, CF), BF16),
        "GHS": ((M, S, CF), BF16),
        "DWI": ((nz, 2, RF, FF), BF16),
        "DWO": ((nz, 2, CF, D), BF16),
        "UPI": ((nz, 2, RF, FF), BF16),
        "UPO": ((nz, 2, CF, D), BF16),
        "DNI": ((nz, 2, RF, FF), BF16),
        "DNO": ((nz, 2, CF, D), BF16),
        "FXI": ((RF, FF), BF16),
        "FXO": ((CF, D), BF16),
        "FYI": ((RF, FF), BF16),
        "FYO": ((CF, D), BF16),
        "GM": ((M, TP, D), F32),
        "GA": ((M, TP, D), BF16),
        "GJ": ((M, TP, 3 * D), BF16),
        "GR": ((8, D), F32),
        "PR": ((D, 128), F32),
        "DG": ((E, nz, 2, RF, TW), BF16),
        "SG": ((nz, 2, RF, 128), BF16),
        "RB1": ((G, nz, 2, RF, TW), BF16),
        "RY1": ((G, h, 2, RF, TW), BF16),
        "RX1": ((G, nz - h, RF, TW), BF16),
        "RX2": ((h, RF, TW), BF16),
        "RY2": ((G, nz - h, RF, TW), BF16),
        "RZ": ((nz, RF, TW), BF16),
        "FIN": ((E, RF, TW), BF16),
        "SH": ((nz, 2, RF, 128), BF16),
        "SB1": ((nz, 2, RF, 128), BF16),
        "SB2": ((G, nz, 2, RF, 128), BF16),
        "SB3": ((nz, RF, 128), BF16),
        "SB4": ((nz, RF, 128), BF16),
    }
    return v


def kernel(c, names, sem_count, *refs):
    nz, E, G, NE, T, TP, CP, S, D, FF, RF, CF, TW, M = (
        c[k]
        for k in ("nz", "E", "G", "NE", "T", "TP", "CP", "S", "D", "FF", "RF", "CF", "TW", "M")
    )
    (xin, cot, routes, qkv_s, out_s, small_s, ein, eout) = refs[:8]
    (act, igrad, gqkv, gout, gsmall, gein, geout) = refs[8:15]
    b = dict(zip(names, refs[15:]))
    SS, RS = refs[-2:]
    h = nz // 2
    nb = D // TW
    nq = 3 * nb
    head = D // HEADS
    pair = 2 * head
    scale = 1.0 / math.sqrt(head)
    sems = Semaphores()
    pending = []

    f = lax.axis_index("fsdp")
    e = lax.axis_index("expert")
    z, x = f // 2, f % 2
    y, core = e // 2, e % 2
    pme = 2 * e + x

    def at(zz, xx, ee):
        return (zz * 2 + xx, ee)

    sibling = at(z, x, y * 2 + (1 - core))
    across = at(z, 1 - x, e)

    def copy_of(src, dst, sem, device):
        return pltpu.make_async_remote_copy(
            src_ref=src,
            dst_ref=dst,
            send_sem=SS.at[sem],
            recv_sem=RS.at[sem],
            device_id=device,
            device_id_type=MESH,
        )

    def when(cond, run):
        if cond is None:
            run()
        else:
            pl.when(cond)(run)

    def send(src, dst, sem, device, cond=None, late=True):
        copy = copy_of(src, dst, sem, device)
        when(cond, copy.start)
        if late:
            pending.append((cond, copy))

    def arrived(dst, sem, cond=None):
        copy = copy_of(dst, dst, sem, sibling)
        when(cond, copy.wait_recv)

    def sent(src, sem, cond=None):
        copy = copy_of(src, src, sem, sibling)
        when(cond, copy.wait_send)

    DW, SM, WIN, WOUT = b["DW"], b["SM"], b["WIN"], b["WOUT"]
    for k in range(nq + nb):

        @pl.when(e == k)
        def _():
            shard = qkv_s if k < nq else out_s
            start = (k % nq) * TW
            DW[k, z, x] = shard[:, start : start + TW]

    SM[z, x] = small_s[...]
    WIN[z, x] = ein[x]
    WOUT[z, x] = eout[x]

    barrier = pltpu.get_barrier_semaphore()
    for dz in range(1, nz):
        pl.semaphore_signal(
            barrier, inc=1, device_id=at((z + dz) % nz, x, e), device_id_type=MESH
        )

    def greet(d, carry):
        p = (pme + d) % NE
        pl.semaphore_signal(barrier, inc=1, device_id=at(z, p % 2, p // 2), device_id_type=MESH)
        return carry

    lax.fori_loop(1, NE, greet, 0)
    pl.semaphore_wait(barrier, nz - 1 + NE - 1)

    s_dz, s_sz = sems.take(nz), sems.take(nz)
    for dz in range(1, nz):
        to = at((z + dz) % nz, x, e)
        send(DW.at[e, z, x], DW.at[e, z, x], s_dz + dz, to)
        send(SM.at[z, x], SM.at[z, x], s_sz + dz, to)

    s_xi, s_xo = sems.take(1), sems.take(1)
    send(ein.at[1 - x], WIN.at[z, x], s_xi, across)

    XP, CT, RT, PM = b["XP"], b["CT"], b["RT"], b["PM"]
    lane = lax.broadcasted_iota(jnp.int32, (TP, 128), 1)
    for m in range(M):
        XP[m] = jnp.zeros((TP, D), BF16)
        CT[m] = jnp.zeros((TP, D), BF16)
        RT[m] = jnp.full((TP, 128), -1, jnp.int32)
        XP[m, 0:T] = xin[m]
        CT[m, 0:T] = cot[m]
        RT[m, 0:T, 0:2] = routes[m]

    def onehot(m, j):
        return RT[m][:, j : j + 1] == lane

    before = (
        lax.broadcasted_iota(jnp.int32, (TP, TP), 1) < lax.broadcasted_iota(jnp.int32, (TP, TP), 0)
    ).astype(BF16)
    place = lax.broadcasted_iota(jnp.int32, (TP, S), 1)
    for m in range(M):
        first = onehot(m, 0).astype(F32)
        second = onehot(m, 1).astype(F32)
        rank0 = nn(before, first.astype(BF16))
        rank1 = nn(before, second.astype(BF16)) + jnp.sum(first, axis=0, keepdims=True)
        for j, (hot, rank) in enumerate(((first, rank0), (second, rank1))):
            slot = jnp.sum(hot * rank, axis=-1, keepdims=True).astype(jnp.int32)
            route = RT[m][:, j : j + 1]
            spot = jnp.where(route >= 0, route * CP + slot, -1)
            PM[m, j] = (place == spot).astype(BF16)

    s_zi = [sems.take(2 * nz), sems.take(2 * nz)]
    s_zo = [sems.take(2 * nz), sems.take(2 * nz)]

    def chain(kind, d, xs=(0, 1)):
        ref, base = (WIN, s_zi) if kind == "in" else (WOUT, s_zo)
        for i in xs:
            xx = x if i == 0 else 1 - x
            up_at, dn_at = z - d, z + d
            if d > 0:
                arrived(ref.at[up_at, xx], base[0] + 2 * d + i, up_at >= 0)
                arrived(ref.at[dn_at, xx], base[1] + 2 * d + i, dn_at < nz)
            if d < nz - 1:
                up_ok = (up_at >= 0) & (z < nz - 1)
                dn_ok = (dn_at < nz) & (z > 0)
                send(
                    ref.at[up_at, xx],
                    ref.at[up_at, xx],
                    base[0] + 2 * (d + 1) + i,
                    at((z + 1) % nz, x, e),
                    up_ok,
                )
                send(
                    ref.at[dn_at, xx],
                    ref.at[dn_at, xx],
                    base[1] + 2 * (d + 1) + i,
                    at((z + nz - 1) % nz, x, e),
                    dn_ok,
                )

    for dz in range(1, nz):
        zz = (z + nz - dz) % nz
        arrived(DW.at[e, zz, x], s_dz + dz)
        arrived(SM.at[zz, x], s_sz + dz)

    s_px, s_psm = sems.take(1), sems.take(1)
    s_py, s_f1, s_f2 = sems.take(G), sems.take(G), sems.take(G)
    s_c = sems.take(2 * G)
    send(DW.at[e, :, x], DW.at[e, :, x], s_px, across)
    send(SM.at[:, x], SM.at[:, x], s_psm, across)
    for d in range(1, G):
        send(DW.at[e, :, x], DW.at[e, :, x], s_py + d, at(z, x, ((y + d) % G) * 2 + core))

    def to_sibling(d, i):
        ee = ((y + G - d) % G) * 2 + core
        xx = x if i == 0 else 1 - x
        send(DW.at[ee, :, xx], DW.at[ee, :, xx], s_c + 2 * d + i, sibling)

    to_sibling(0, 0)
    chain("in", 0, (0,))
    arrived(WIN.at[z, 1 - x], s_xi)
    chain("in", 0, (1,))
    arrived(DW.at[e, :, 1 - x], s_px)
    for d in range(1, G):
        to = at(z, x, ((y + d) % G) * 2 + core)
        send(DW.at[e, 0:h, 1 - x], DW.at[e, 0:h, 1 - x], s_f1 + d, to)
    to_sibling(0, 1)
    for d in range(1, G):
        ee = ((y + G - d) % G) * 2 + core
        arrived(DW.at[ee, :, x], s_py + d)
        send(DW.at[ee, h:nz, x], DW.at[ee, h:nz, x], s_f2 + d, across)
        to_sibling(d, 0)
    for d in range(1, G):
        ee = ((y + G - d) % G) * 2 + core
        arrived(DW.at[ee, 0:h, 1 - x], s_f1 + d)
        arrived(DW.at[ee, h:nz, 1 - x], s_f2 + d)
        to_sibling(d, 1)
    send(eout.at[1 - x], WOUT.at[z, x], s_xo, across)
    arrived(SM.at[:, 1 - x], s_psm)
    for d in range(G):
        ee = ((y + G - d) % G) * 2 + (1 - core)
        arrived(DW.at[ee, :, x], s_c + 2 * d)
        arrived(DW.at[ee, :, 1 - x], s_c + 2 * d + 1)

    chain("in", 1)

    def dense(k):
        return DW[k].reshape(D, TW)

    small = SM[...].reshape(D, 128)
    row = lax.broadcasted_iota(jnp.int32, (8, 128), 0)
    col = lax.broadcasted_iota(jnp.int32, (8, 128), 1)
    pick = (((row == 0) & (col == 126)) | ((row == 1) & (col == 127))).astype(BF16)
    gains = nt(pick, small)
    gain_one, gain_two = gains[0:1], gains[1:2]
    key_ok = lax.broadcasted_iota(jnp.int32, (1, TP), 1) < T
    low_half = lax.broadcasted_iota(jnp.int32, (1, pair), 1) < head
    N1, J, ATT, MID, N2 = b["N1"], b["J"], b["ATT"], b["MID"], b["N2"]
    GATES, XGS, XG = b["GATES"], b["XGS"], b["XG"]

    def half_of(value, i):
        keep = low_half if i == 0 else jnp.logical_not(low_half)
        return jnp.where(keep, value, jnp.zeros_like(value))

    def softmax_scores(query, keys):
        scores = jnp.where(key_ok, nt(query, keys) * scale, -1e30)
        raised = jnp.exp(scores - jnp.max(scores, axis=-1, keepdims=True))
        return raised * (1.0 / jnp.sum(raised, axis=-1, keepdims=True))

    def columns(base, hp):
        return pl.ds(pl.multiple_of(base + hp * pair, 128), pair)

    def chosen_of(m, j):
        gates = GATES[m]
        return jnp.sum(jnp.where(onehot(m, j), gates, 0.0), axis=-1, keepdims=True)

    def forward(m):
        tokens = XP[m].astype(F32)
        hat, _ = normalize(tokens)
        N1[m] = (hat * gain_one).astype(BF16)
        for k in range(nq):
            J[m, :, k * TW : (k + 1) * TW] = nn(N1[m], dense(k)).astype(BF16)

        def attend(hp, carry):
            query, keys, values = (J[m, :, columns(i * D, hp)] for i in range(3))
            total = jnp.zeros((TP, pair), F32)
            for i in range(2):
                probs = softmax_scores(half_of(query, i), keys).astype(BF16)
                total = total + nn(probs, half_of(values, i))
            ATT[m, :, columns(0, hp)] = total.astype(BF16)
            return carry

        lax.fori_loop(0, D // pair, attend, 0)
        for k in range(nb):
            cols = slice(k * TW, (k + 1) * TW)
            MID[m, :, cols] = XP[m, :, cols].astype(F32) + nn(ATT[m], dense(nq + k))
        hat, _ = normalize(MID[m])
        N2[m] = (hat * gain_two).astype(BF16)
        logits = jnp.where(lane < NE, nn(N2[m], small), -1e30)
        raised = jnp.exp(logits - jnp.max(logits, axis=-1, keepdims=True))
        GATES[m] = raised / jnp.sum(raised, axis=-1, keepdims=True)
        upstream = CT[m].astype(F32)
        XGS[m, 0] = tn(PM[m, 0] + PM[m, 1], N2[m]).astype(BF16).reshape(NE, CP, D)
        placed = tn(PM[m, 0], (chosen_of(m, 0) * upstream).astype(BF16))
        placed = placed + tn(PM[m, 1], (chosen_of(m, 1) * upstream).astype(BF16))
        XGS[m, 1] = placed.astype(BF16).reshape(NE, CP, D)

    def exchange(src, dst, m, base):
        def one(d, carry):
            p = (pme + d) % NE
            copy_of(
                src.at[m, :, p], dst.at[m, :, pme], base + d, at(z, p % 2, p // 2)
            ).start()
            return carry

        lax.fori_loop(1, NE, one, 0)
        dst[m, :, pme] = src[m, :, pme]

    def exchanged(src, dst, m, base):
        def one(d, carry):
            p = (pme + NE - d) % NE
            copy_of(dst.at[m, :, p], dst.at[m, :, p], base + d, sibling).wait_recv()
            return carry

        lax.fori_loop(1, NE, one, 0)

    def exchange_sent(src, m, base):
        def one(d, carry):
            p = (pme + d) % NE
            copy_of(src.at[m, :, p], src.at[m, :, p], base + d, sibling).wait_send()
            return carry

        lax.fori_loop(1, NE, one, 0)

    s_go = [sems.take(NE) for _ in range(M)]
    s_back = [sems.take(NE) for _ in range(M)]
    for m in range(M):
        forward(m)
        exchange(XGS, XG, m, s_go[m])
        if m == 0:
            chain("in", 2) if nz > 2 else None
            chain("out", 0, (0,))
            arrived(WOUT.at[z, 1 - x], s_xo)
            chain("out", 0, (1,))
    for d in range(3, nz):
        chain("in", d)
    chain("out", 1)
    for m in range(M):
        exchanged(XGS, XG, m, s_go[m])

    YACC, DXACC, AS, GHS = b["YACC"], b["DXACC"], b["AS"], b["GHS"]
    DWI, DWO = b["DWI"], b["DWO"]
    YACC[...] = jnp.zeros_like(YACC)
    DXACC[...] = jnp.zeros_like(DXACC)
    c0, c1 = math.sqrt(2.0 / math.pi), 0.044715

    def expert_block(zc):
        for xx in range(2):
            cols = pl.ds(pl.multiple_of((2 * zc + xx) * CF, CF), CF)
            w_in = WIN[:, :, :, cols].reshape(D, CF)
            w_out = WOUT[zc, xx]

            def part(m, carry):
                tokens = XG[m, 0].reshape(S, D)
                grads = XG[m, 1].reshape(S, D)
                hidden = nn(tokens, w_in)
                grad_acted = nt(grads, w_out)
                square = hidden * hidden
                bent = jnp.tanh(c0 * hidden * (1.0 + c1 * square))
                acted = (0.5 * hidden * (1.0 + bent)).astype(BF16)
                slope = 0.5 * (1.0 + bent) + 0.5 * c0 * hidden * (1.0 - bent * bent) * (
                    1.0 + 3.0 * c1 * square
                )
                grad_hidden = (grad_acted * slope).astype(BF16)
                AS[m] = acted
                GHS[m] = grad_hidden
                YACC[m] = YACC[m] + nn(acted, w_out)
                DXACC[m] = DXACC[m] + nt(grad_hidden, w_in)
                return carry

            lax.fori_loop(0, M, part, 0)
            grads = XG[:, 1].reshape(M * S, D)
            tokens = XG[:, 0].reshape(M * S, D)
            DWO[zc, xx] = tn(AS[...].reshape(M * S, CF), grads).astype(BF16)
            DWI[:, :, :, cols] = (
                tn(tokens, GHS[...].reshape(M * S, CF)).astype(BF16).reshape(nz, 2, RF, CF)
            )

    turn = 1 - 2 * (z // h)
    for i in range(nz):
        if i >= 1:
            if i + 1 < nz:
                chain("out", i + 1)
        expert_block((z + turn * i + nz) % nz)

    YD, RET = b["YD"], b["RET"]
    for m in range(M):
        YD[m, 0] = YACC[m].astype(BF16).reshape(NE, CP, D)
        YD[m, 1] = DXACC[m].astype(BF16).reshape(NE, CP, D)
        exchange(YD, RET, m, s_back[m])

    UP, DN = (b["UPI"], b["UPO"]), (b["DNI"], b["DNO"])
    OWN = (DWI, DWO)
    s_up, s_dn = sems.take(4 * nz), sems.take(4 * nz)
    rounds = 2 * (nz - 1)

    def sums(r0, r1):
        def step(r, carry):
            for side, (got, base) in enumerate(((UP, s_up), (DN, s_dn))):
                place_z = z if side == 0 else nz - 1 - z
                j = r - place_z
                goal = nz - 1 - (j + 2 * nz) // 2 + nz
                ok = (j >= 0) & (goal > place_z)
                goal = goal if side == 0 else nz - 1 - goal
                goal = jnp.clip(goal, 0, nz - 1)
                xx = (1 - x + j + 2 * nz) % 2
                to = at((z + 1) % nz if side == 0 else (z + nz - 1) % nz, x, e)

                @pl.when(ok)
                def _():
                    for kind in range(2):
                        sem = base + 4 * goal + 2 * kind + xx

                        @pl.when(place_z > 0)
                        def _():
                            arrived(got[kind].at[goal, xx], sem)
                            OWN[kind][goal, xx] = OWN[kind][goal, xx] + got[kind][goal, xx]

                        copy_of(
                            OWN[kind].at[goal, xx], got[kind].at[goal, xx], sem, to
                        ).start()

            return carry

        lax.fori_loop(r0, r1, step, 0)

    s_fin = sems.take(2)
    FX, FY = (b["FXI"], b["FXO"]), (b["FYI"], b["FYO"])
    GE = (gein, geout)

    def sums_end():
        for kind in range(2):
            for i in range(2):
                xx = 1 - x if i == 0 else x
                up_sem = s_up + 4 * z + 2 * kind + xx
                dn_sem = s_dn + 4 * z + 2 * kind + xx
                arrived(UP[kind].at[z, xx], up_sem, z > 0)
                arrived(DN[kind].at[z, xx], dn_sem, z < nz - 1)

                @pl.when(z == 0)
                def _():
                    UP[kind][z, xx] = jnp.zeros(UP[kind].shape[2:], BF16)

                @pl.when(z == nz - 1)
                def _():
                    DN[kind][z, xx] = jnp.zeros(DN[kind].shape[2:], BF16)

                total = (
                    OWN[kind][z, xx].astype(F32)
                    + UP[kind][z, xx].astype(F32)
                    + DN[kind][z, xx].astype(F32)
                )
                if i == 0:
                    FX[kind][...] = total.astype(BF16)
                    send(FX[kind], FY[kind], s_fin + kind, across)
                else:
                    GE[kind][x] = total
        for kind in range(2):
            arrived(FY[kind], s_fin + kind)
            GE[kind][1 - x] = FY[kind][...].astype(F32)

        def clear(r, carry):
            for side, (got, base) in enumerate(((UP, s_up), (DN, s_dn))):
                place_z = z if side == 0 else nz - 1 - z
                goal = r // 2
                ok = (goal > z) if side == 0 else (goal < z)

                @pl.when(ok)
                def _():
                    for kind in range(2):
                        sent(OWN[kind].at[goal, r % 2], base + 4 * goal + 2 * kind + r % 2)

            return carry

        lax.fori_loop(0, 2 * nz, clear, 0)

    GM, GA, GJ, GR, PR = b["GM"], b["GA"], b["GJ"], b["GR"], b["PR"]
    DG, SG = b["DG"], b["SG"]
    GR[...] = jnp.zeros_like(GR)

    def backward_top(m):
        result = RET[m, 0].reshape(S, D)
        picked0 = nn(PM[m, 0], result)
        picked1 = nn(PM[m, 1], result)
        out = MID[m] + chosen_of(m, 0) * picked0 + chosen_of(m, 1) * picked1
        act[m] = out[0:T].astype(BF16)
        upstream = CT[m].astype(F32)
        gates = GATES[m]
        grad_gates = jnp.where(
            onehot(m, 0), jnp.sum(upstream * picked0, axis=-1, keepdims=True), 0.0
        ) + jnp.where(onehot(m, 1), jnp.sum(upstream * picked1, axis=-1, keepdims=True), 0.0)
        grad_logits = (
            gates * (grad_gates - jnp.sum(grad_gates * gates, axis=-1, keepdims=True))
        ).astype(BF16)
        router_part = tn(N2[m], grad_logits)
        PR[...] = router_part if m == 0 else PR[...] + router_part
        grad = nn(PM[m, 0] + PM[m, 1], RET[m, 1].reshape(S, D)) + nt(grad_logits, small)
        hat, rstd = normalize(MID[m])
        GR[1:2] = GR[1:2] + jnp.sum(grad * hat, axis=0, keepdims=True)
        grad_middle = upstream + normalize_back(grad * gain_two, hat, rstd)
        GM[m] = grad_middle
        branch = grad_middle.astype(BF16)
        N2[m] = branch
        back = None
        for k in range(nb):
            term = nt(branch[:, k * TW : (k + 1) * TW], dense(nq + k))
            back = term if back is None else back + term
        GA[m] = back.astype(BF16)

    def backward_heads(m):
        def attend(hp, carry):
            query, keys, values = (J[m, :, columns(i * D, hp)] for i in range(3))
            grads = GA[m, :, columns(0, hp)]
            grad_query = jnp.zeros((TP, pair), F32)
            grad_keys = jnp.zeros((TP, pair), F32)
            grad_values = jnp.zeros((TP, pair), F32)
            for i in range(2):
                part = half_of(query, i)
                upstream = half_of(grads, i)
                probs = softmax_scores(part, keys)
                grad_probs = nt(upstream, values)
                grad_values = grad_values + tn(probs.astype(BF16), upstream)
                grad_scores = (
                    probs
                    * (grad_probs - jnp.sum(grad_probs * probs, axis=-1, keepdims=True))
                ).astype(BF16)
                grad_query = grad_query + nn(grad_scores, half_of(keys, i))
                grad_keys = grad_keys + tn(grad_scores, part)
            GJ[m, :, columns(0, hp)] = (grad_query * scale).astype(BF16)
            GJ[m, :, columns(D, hp)] = (grad_keys * scale).astype(BF16)
            GJ[m, :, columns(2 * D, hp)] = grad_values.astype(BF16)
            return carry

        lax.fori_loop(0, D // pair, attend, 0)

    def backward_end(m):
        grad = None
        for k in range(nq):
            term = nt(GJ[m, :, k * TW : (k + 1) * TW], dense(k))
            grad = term if grad is None else grad + term
        hat, rstd = normalize(XP[m].astype(F32))
        GR[0:1] = GR[0:1] + jnp.sum(grad * hat, axis=0, keepdims=True)
        full = GM[m] + normalize_back(grad * gain_one, hat, rstd)
        igrad[m] = full[0:T]

    for m in range(M):
        exchanged(YD, RET, m, s_back[m])
        backward_top(m)
        sums(m, m + 1)
    for k in range(nb):
        part = tn(
            ATT[...].reshape(M * TP, D), N2[:, :, k * TW : (k + 1) * TW].reshape(M * TP, TW)
        )
        DG[nq + k] = part.astype(BF16).reshape(nz, 2, RF, TW)
    for m in range(M):
        backward_heads(m)
        sums(M + m, M + m + 1)
    for k in range(nq):
        part = tn(
            N1[...].reshape(M * TP, D), GJ[:, :, k * TW : (k + 1) * TW].reshape(M * TP, TW)
        )
        DG[k] = part.astype(BF16).reshape(nz, 2, RF, TW)
    for m in range(M):
        backward_end(m)
    gain_part = tn(GR[...].astype(BF16), pick)
    SG[...] = (PR[...] + gain_part).astype(BF16).reshape(nz, 2, RF, 128)

    RB1, RY1, RX1, RX2, RY2, RZ, FIN = (
        b[k] for k in ("RB1", "RY1", "RX1", "RX2", "RY2", "RZ", "FIN")
    )
    SH, SB1, SB2, SB3, SB4 = (b[k] for k in ("SH", "SB1", "SB2", "SB3", "SB4"))
    s_r1, s_ry1, s_rx1 = sems.take(G), sems.take(G), sems.take(G)
    s_rx2, s_ry2, s_rz, s_fe = sems.take(1), sems.take(G), sems.take(nz), sems.take(E)
    s_b1, s_b2, s_b3, s_b4 = sems.take(1), sems.take(G), sems.take(1), sems.take(nz)
    for j in range(G):
        send(DG.at[2 * j + 1 - core], RB1.at[j], s_r1 + j, sibling)
    send(SG, SB1, s_b1, sibling)
    for j in range(G):
        arrived(RB1.at[j], s_r1 + j)
        DG[2 * j + core] = DG[2 * j + core] + RB1[j]
    arrived(SB1, s_b1)
    SB2[y] = SG[...] + SB1[...]
    for d in range(1, G):
        q = (y + d) % G
        send(DG.at[2 * q + core, 0:h], RY1.at[y], s_ry1 + d, at(z, x, 2 * q + core))
        send(SB2.at[y], SB2.at[y], s_b2 + d, at(z, x, 2 * q + core))
    for j in range(G):
        send(DG.at[2 * j + core, h:nz, 1 - x], RX1.at[j], s_rx1 + j, across)
    sums(2 * M, 2 * M + 1) if rounds > 2 * M else None
    for d in range(1, G):
        q = (y + G - d) % G
        arrived(RY1.at[q], s_ry1 + d)
        DG[e, 0:h] = DG[e, 0:h] + RY1[q]
    send(DG.at[e, 0:h, 1 - x], RX2, s_rx2, across)
    for j in range(G):
        arrived(RX1.at[j], s_rx1 + j)
        DG[2 * j + core, h:nz, x] = DG[2 * j + core, h:nz, x] + RX1[j]
    for d in range(1, G):
        q = (y + d) % G
        send(DG.at[2 * q + core, h:nz, x], RY2.at[y], s_ry2 + d, at(z, x, 2 * q + core))
    for d in range(1, G):
        arrived(SB2.at[(y + G - d) % G], s_b2 + d)
    total = SB2[0].astype(F32)
    for j in range(1, G):
        total = total + SB2[j].astype(F32)
    SH[...] = total.astype(BF16)
    send(SH.at[:, 1 - x], SB3, s_b3, across)
    arrived(RX2, s_rx2)
    DG[e, 0:h, x] = DG[e, 0:h, x] + RX2[...]
    for d in range(1, G):
        q = (y + G - d) % G
        arrived(RY2.at[q], s_ry2 + d)
        DG[e, h:nz, x] = DG[e, h:nz, x] + RY2[q]
    for dz in range(1, nz):
        zz = (z + dz) % nz
        send(DG.at[e, zz, x], RZ.at[z], s_rz + dz, at(zz, x, e))
    arrived(SB3, s_b3)
    SH[:, x] = SH[:, x] + SB3[...]
    for dz in range(1, nz):
        zz = (z + dz) % nz
        send(SH.at[zz, x], SB4.at[z], s_b4 + dz, at(zz, x, e))
    for r in range(2 * M + 1, rounds):
        sums(r, r + 1)
    RZ[z] = DG[e, z, x]
    for dz in range(1, nz):
        arrived(RZ.at[(z + nz - dz) % nz], s_rz + dz)
    total = RZ[0].astype(F32)
    for k in range(1, nz):
        total = total + RZ[k].astype(F32)
    FIN[e] = total.astype(BF16)

    def spread(d, carry):
        copy_of(FIN.at[e], FIN.at[e], s_fe + d, at(z, x, (e + d) % E)).start()
        return carry

    lax.fori_loop(1, E, spread, 0)
    SB4[z] = SH[z, x]
    for dz in range(1, nz):
        arrived(SB4.at[(z + nz - dz) % nz], s_b4 + dz)
    total = SB4[0].astype(F32)
    for k in range(1, nz):
        total = total + SB4[k].astype(F32)
    gsmall[...] = total
    sums_end()

    def spread_done(d, carry):
        ee = (e + E - d) % E
        copy_of(FIN.at[ee], FIN.at[ee], s_fe + d, sibling).wait_recv()
        return carry

    lax.fori_loop(1, E, spread_done, 0)
    for k in range(nq):
        gqkv[:, k * TW : (k + 1) * TW] = FIN[k].astype(F32)
    for k in range(nb):
        gout[:, k * TW : (k + 1) * TW] = FIN[nq + k].astype(F32)

    for m in range(M):
        exchange_sent(XGS, m, s_go[m])
        exchange_sent(YD, m, s_back[m])

    def spread_sent(d, carry):
        copy_of(FIN.at[e], FIN.at[e], s_fe + d, sibling).wait_send()
        return carry

    lax.fori_loop(1, E, spread_sent, 0)
    for cond, copy in pending:
        when(cond, copy.wait_send)
    assert sems.used <= sem_count, sems.used


def body(
    mesh_shape,
    inputs,
    gain_attn,
    qkv_weight,
    out_weight,
    gain_moe,
    router_weight,
    expert_in,
    expert_out,
    routes,
    cotangent,
):
    micro, images, seq, width = inputs.shape
    c = layout(mesh_shape, micro, images * seq, width, expert_in.shape[2])
    rows, columns = images * seq, c["NE"]
    small = jnp.concatenate(
        [
            router_weight,
            jnp.zeros((c["RF"], 126 - columns), BF16),
            gain_attn[:, None],
            gain_moe[:, None],
        ],
        axis=1,
    )
    scratch = scratch_of(c)
    names = list(scratch)
    sem_count = 40 + 20 * c["nz"] + 8 * c["G"] + 4 * c["NE"] + c["E"]
    vmem = pl.BlockSpec(memory_space=pltpu.VMEM)
    shapes = (
        ((micro, rows, width), BF16),
        ((micro, rows, width), F32),
        (qkv_weight.shape, F32),
        (out_weight.shape, F32),
        ((c["RF"], 128), F32),
        (expert_in.shape, F32),
        (expert_out.shape, F32),
    )
    act, igrad, gqkv, gout, gsmall, gein, geout = pl.pallas_call(
        functools.partial(kernel, c, names, sem_count),
        out_shape=[jax.ShapeDtypeStruct(s, t) for s, t in shapes],
        in_specs=[vmem] * 8,
        out_specs=[vmem] * 7,
        scratch_shapes=[pltpu.VMEM(s, t) for s, t in scratch.values()]
        + [pltpu.SemaphoreType.DMA((sem_count,)), pltpu.SemaphoreType.DMA((sem_count,))],
        compiler_params=pltpu.CompilerParams(
            collective_id=0, has_side_effects=True, vmem_limit_bytes=60 * 1024 * 1024
        ),
    )(
        inputs.reshape(micro, rows, width),
        cotangent.reshape(micro, rows, width),
        routes.reshape(micro, rows, 2),
        qkv_weight,
        out_weight,
        small,
        expert_in,
        expert_out,
    )
    return (
        act.reshape(inputs.shape),
        igrad.reshape(inputs.shape),
        gsmall[:, 126],
        gqkv,
        gout,
        gsmall[:, 127],
        gsmall[:, :columns],
        gein,
        geout,
    )


def solution(mesh):
    return jax.shard_map(
        functools.partial(body, dict(mesh.shape)),
        mesh=mesh,
        in_specs=(
            P(None, ("fsdp", "expert"), None, None),
            P("fsdp"),
            P("fsdp", None),
            P("fsdp", None),
            P("fsdp"),
            P("fsdp", None),
            P("expert", "fsdp", None),
            P("expert", "fsdp", None),
            P(None, ("fsdp", "expert"), None, None),
            P(None, ("fsdp", "expert"), None, None),
        ),
        out_specs=(
            P(None, ("fsdp", "expert"), None, None),
            P(None, ("fsdp", "expert"), None, None),
            P("fsdp"),
            P("fsdp", None),
            P("fsdp", None),
            P("fsdp"),
            P("fsdp", None),
            P("expert", "fsdp", None),
            P("expert", "fsdp", None),
        ),
        check_vma=False,
    )
```

time: 828 us -> 209 us (0.25); the launches traced: 816 us -> 209 us
  waiting for transfers between devices: 387 us -> 0 us
  Pallas kernels: 0 us -> 193 us
  blocking collectives: 107 us -> 0 us
  matrix products: 104 us -> 0 us
  local copies, waits for them, and re-layouts: 115 us -> 14.5 us
  other arithmetic: 53.3 us -> 0.69 us
  starting transfers between devices: 33.2 us -> 0 us
  between operations: 17 us -> 0.69 us
    reduce_scatter x4 -> x0, waiting for transfers between devices: 291 us -> none  [the longest x1 89.2 us: body(): lax.psum_scatter(totals[6].astype(jnp.bfloat16), 'fsdp', scatter_dimensio...]
    pallas_call x0 -> x1, Pallas kernels: none -> 193 us  [body(): pl.pallas_call(functools.partial(kernel, c, names, sem_count), out_shape=...]
    dot_general x42 -> x0, matrix products: 104 us -> none  [the longest x2 13.7 us: body(): jnp.einsum('ecd,edf->ecf', arrived, first_w, preferred_element_type=jnp.f...]
    all_gather x2 -> x0, blocking collectives: 58.9 us -> none  [the longest x1 32.7 us: body(): lax.all_gather(out_weight, 'fsdp', axis=0, tiled=True)]
    unnamed x2 -> x0, blocking collectives: 42.5 us -> none
    all_gather x3 -> x0, waiting for transfers between devices: 38.6 us -> none  [the longest x1 38.6 us: body(): lax.all_gather(expert_in, 'fsdp', axis=1, tiled=True)]
    all_to_all x8 -> x0, starting transfers between devices: 32.4 us -> none  [the longest x2 8.68 us: body(): lax.all_to_all(produced, 'expert', split_axis=1, concat_axis=0, tiled=True)]
    psum x1 -> x0, waiting for transfers between devices: 25.5 us -> none  [body(): lax.psum(summed[1].astype(jnp.bfloat16), 'expert').astype(jnp.float32)]
  transfers between devices with their start and end apart: 17 -> 0, of which waited for: 11 -> 0; matrix products, arithmetic and copies ran while one was open for 19% -> 0% of each run, Pallas kernels for 0% -> 0%
where the time goes in v1:
time: 209 us
  Pallas kernels  193 us (92%)
  local copies, waits for them, and re-layouts  14.5 us (7%)
    pallas_call x1, Pallas kernels, body(): pl.pallas_call(functools.partial(kernel, c, names, sem_count), out_shape=...  193 us
    unnamed x29, local copies, waits for them, and re-layouts  11.4 us

profile of v1, /device:TPU:0, one launch (start us, length us, event | category | flops | bytes accessed | tf_op | source)
XLA Modules:
  0.0 208.7 jit_solution(9870088961888054472)
XLA Ops:
  0.7 0.0 copy-start.8
  0.7 0.1 pad.1.clone
  0.7 0.6 copy-done.8
  1.3 0.0 copy-start.9
  1.3 0.1 copy.32
  1.4 0.5 copy-done.9
  2.0 0.0 copy-start.7
  2.0 0.1 copy.33
  2.1 0.6 copy-done.7
  2.6 0.1 copy.31
  2.7 0.0 copy-start.6
  2.8 0.7 pad_maximum_fusion.refs_5_
  3.4 0.0 copy-done.6
  3.4 0.8 copy.30
  4.3 2.1 %copy_bitcast_fusion = (bf16[2,197,512]{2,1,0:T(8,128)(2,1)}, bf16[2,197,512]{2,1,0:T(8,128)(2,1)}) fusion(bf16[2,1,197,512]{3,0,2,1:T(2,128)(2,1)} %param.19, bf16[2,1,197,512]{3,0,2,1:T(2,128)(2,1)} %param.10), kind=kLoop, calls=%fused_computation | loop fusion | bytes 1613824 | tf_op jit(solution)/shard_map/reshape | solution.py:820
  6.4 192.8 %shard_map.169 = (bf16[2,197,512]{2,1,0:T(8,128)(2,1)}, f32[2,197,512]{2,1,0:T(8,128)}, f32[64,1536]{1,0:T(8,128)}, f32[64,512]{1,0:T(8,128)}, f32[64,128]{1,0:T...) custom-call(bf16[2,197,512]{2,1,0:T(8,128)(2,1)} %get-tuple-element.44.refs_0_, ...), custom_call_target="tpu_custom_call" | custom-call | tf_op jit(solution)/shard_map/pallas_call | solution.py:808
  199.2 0.0 copy-start.2
  199.2 2.1 %copy.34 = bf16[2,1,197,512]{3,0,2,1:T(2,128)(2,1)} copy(bf16[2,1,197,512]{3,2,0,1:T(8,128)(2,1)} %bitcast.12) | data formatting | bytes 806912
  201.3 0.0 copy-done.2
  201.3 0.0 copy-start.4
  201.3 0.0 copy-start.3
  201.3 0.0 copy-start.1
  201.4 1.7 copy.35
  203.1 0.0 copy-done.4
  203.1 0.7 slice_reduce_fusion
  203.8 0.7 copy.36
  204.4 0.0 copy-done.3
  204.4 0.0 copy-start.5
  204.4 0.7 copy.43
  205.2 0.3 copy-done.5
  205.5 0.7 copy.44
  206.1 0.0 copy-done.1
  206.1 0.0 copy-start
  206.1 1.0 copy.45
  207.1 0.6 copy-done
  207.7 1.0 copy.46
  (1 shorter events, 0.0 us)
Async XLA Ops:
  0.7 0.7 copy-start.8
  1.3 0.7 copy-start.9
  2.0 0.7 copy-start.7
  2.7 0.7 copy-start.6
  199.2 2.1 %copy-start.2 = (f32[2,197,512]{2,1,0:T(8,128)S(1)}, f32[2,197,512]{2,1,0:T(8,128)}, u32[]{:S(2)}) copy-start(f32[2,197,512]{2,1,0:T(8,128)} %get-tuple-element.17) | copy-start | bytes 2420740
  201.3 1.7 copy-start.4
  201.3 3.1 %copy-start.3 = (f32[64,1536]{1,0:T(8,128)S(1)}, f32[64,1536]{1,0:T(8,128)}, u32[]{:S(2)}) copy-start(f32[64,1536]{1,0:T(8,128)} %get-tuple-element.57) | copy-start | bytes 1179652
  201.3 4.8 %copy-start.1 = (f32[2,64,2048]{2,1,0:T(8,128)S(1)}, f32[2,64,2048]{2,1,0:T(8,128)}, u32[]{:S(2)}) copy-start(f32[2,64,2048]{2,1,0:T(8,128)} %get-tuple-element.61) | copy-start | bytes 3145732
  204.4 1.0 copy-start.5
  206.1 1.6 copy-start

commit v2 on v1

v2 whole, which is shorter than its diff:
```python
import functools
import math

import jax
import jax.numpy as jnp
from jax import lax
from jax.experimental import pallas as pl
from jax.experimental.pallas import tpu as pltpu
from jax.sharding import PartitionSpec as P

HEADS = 8
EPS = 1e-06
MESH = pl.DeviceIdType.MESH
F32 = jnp.float32
BF16 = jnp.bfloat16


def nn(a, b):
    return lax.dot_general(a, b, (((1,), (0,)), ((), ())), preferred_element_type=F32)


def nt(a, b):
    return lax.dot_general(a, b, (((1,), (1,)), ((), ())), preferred_element_type=F32)


def tn(a, b):
    return lax.dot_general(a, b, (((0,), (0,)), ((), ())), preferred_element_type=F32)


def normalize(values):
    center = jnp.mean(values, axis=-1, keepdims=True)
    shifted = values - center
    spread = jnp.mean(shifted * shifted, axis=-1, keepdims=True)
    rstd = lax.rsqrt(spread + EPS)
    return shifted * rstd, rstd


def normalize_back(grad, hat, rstd):
    return rstd * (
        grad
        - jnp.mean(grad, axis=-1, keepdims=True)
        - hat * jnp.mean(grad * hat, axis=-1, keepdims=True)
    )


class Semaphores:
    def __init__(self):
        self.used = 0

    def take(self, count):
        start = self.used
        self.used += count
        return start


SIZES = ("nz", "E", "G", "NE", "NR", "T", "TP", "CP", "S", "D", "FC", "RF", "CF", "TW", "M")


def layout(mesh_shape, micro, seq, width, ff_width):
    fsdp, peers = mesh_shape["fsdp"], mesh_shape["expert"]
    c = {}
    c["nz"] = fsdp // 2
    c["E"] = peers
    c["G"] = peers // 2
    c["NE"] = 2 * peers
    c["T"] = seq
    c["TP"] = -(-seq // 16) * 16
    c["CP"] = -(-max(2, 10 * seq // (4 * 2 * peers) + 1) // 16) * 16
    c["S"] = c["NE"] * c["CP"]
    c["NR"] = -(-(c["NE"] + 2) // 16) * 16
    c["D"] = width
    c["FF"] = ff_width
    c["RF"] = width // fsdp
    c["CF"] = ff_width // fsdp
    c["FC"] = 2 * c["CF"]
    c["TW"] = 4 * width // peers
    c["M"] = micro
    return c


def scratch_of(c):
    nz, E, G, NE, NR, T, TP, CP, S, D, FC, RF, CF, TW, M = (c[k] for k in SIZES)
    h = nz // 2
    v = {
        "XP": ((M, TP, D), BF16),
        "CT": ((M, TP, D), BF16),
        "XR": ((T, M, D), BF16),
        "CR": ((T, M, D), BF16),
        "AR": ((T, M, D), F32),
        "AO": ((T, M, D), BF16),
        "IG": ((M, T, 1, D), F32),
        "RR": ((M, 2, T), jnp.int32),
        "RT": ((M, TP, 128), F32),
        "SR": ((nz, 2, NR, RF), BF16),
        "G1": ((1, RF), BF16),
        "G2": ((1, RF), BF16),
        "RW": ((NE, RF), BF16),
        "GQ": ((RF, 3 * D), F32),
        "GO": ((RF, D), F32),
        "GI": ((2, RF, nz * FC), F32),
        "GT": ((2, CF, D), F32),
        "GS": ((NR, RF), F32),
        "DW": ((E, nz, 2, RF, TW), BF16),
        "SM": ((nz, 2, RF, 128), BF16),
        "WIN": ((nz, nz, 2, RF, FC), BF16),
        "WOUT": ((nz, 2, CF, D), BF16),
        "N1": ((M, TP, D), BF16),
        "J": ((M, TP, 3 * D), BF16),
        "ATT": ((M, TP, D), BF16),
        "MID": ((M, TP, D), F32),
        "N2": ((M, TP, D), BF16),
        "GATES": ((M, TP, 128), F32),
        "PM": ((M, 2, TP, S), BF16),
        "XGS": ((M, 2, NE, CP, D), BF16),
        "XG": ((M, 2, NE, CP, D), BF16),
        "YD": ((M, 2, NE, CP, D), BF16),
        "RET": ((M, 2, NE, CP, D), BF16),
        "YACC": ((M, S, D), F32),
        "DXACC": ((M, S, D), F32),
        "AS": ((M, S, FC), BF16),
        "GHS": ((M, S, FC), BF16),
        "DWI": ((nz, nz, 2, RF, FC), BF16),
        "DWO": ((nz, 2, CF, D), BF16),
        "UPI": ((nz, nz, 2, RF, FC), BF16),
        "UPO": ((nz, 2, CF, D), BF16),
        "DNI": ((nz, nz, 2, RF, FC), BF16),
        "DNO": ((nz, 2, CF, D), BF16),
        "FXI": ((nz, RF, FC), BF16),
        "FXO": ((CF, D), BF16),
        "FYI": ((nz, RF, FC), BF16),
        "FYO": ((CF, D), BF16),
        "GM": ((M, TP, D), F32),
        "GA": ((M, TP, D), BF16),
        "GJ": ((M, TP, 3 * D), BF16),
        "GR": ((NR, D), F32),
        "DG": ((E, nz, 2, RF, TW), BF16),
        "RB1": ((G, nz, 2, RF, TW), BF16),
        "RY1": ((G, h, 2, RF, TW), BF16),
        "RX1": ((G, nz - h, RF, TW), BF16),
        "RX2": ((h, RF, TW), BF16),
        "RY2": ((G, nz - h, RF, TW), BF16),
        "RZ": ((nz, RF, TW), BF16),
        "FIN": ((E, RF, TW), BF16),
        "GB": ((NR, D), BF16),
        "SB1": ((NR, D), BF16),
        "SB2": ((G, NR, D), BF16),
        "SB3": ((2, NR, D), BF16),
        "SB4": ((nz, NR, D), BF16),
    }
    return v


def kernel(c, names, counts, *refs):
    nz, E, G, NE, NR, T, TP, CP, S, D, FC, RF, CF, TW, M = (c[k] for k in SIZES)
    (xin, cot, routes, qkv_s, out_s, gain1, gain2, router, ein, eout) = refs[:10]
    (act, igrad, gqkv, gout, ggain1, ggain2, grouter, gein, geout) = refs[10:19]
    b = dict(zip(names, refs[19:]))
    SS, RS, LS = refs[-3:]
    h = nz // 2
    nb = D // TW
    nq = 3 * nb
    head = D // HEADS
    pair = 2 * head
    scale = 1.0 / math.sqrt(head)
    sems, sends, locals_ = Semaphores(), Semaphores(), Semaphores()
    pending = []

    f = lax.axis_index("fsdp")
    e = lax.axis_index("expert")
    z, x = f // 2, f % 2
    y, core = e // 2, e % 2
    pme = 2 * e + x

    def at(zz, xx, ee):
        return (zz * 2 + xx, ee)

    sibling = at(z, x, y * 2 + (1 - core))
    across = at(z, 1 - x, e)

    def copy_of(src, dst, ssem, rsem, device):
        return pltpu.make_async_remote_copy(
            src_ref=src,
            dst_ref=dst,
            send_sem=SS.at[ssem],
            recv_sem=RS.at[rsem],
            device_id=device,
            device_id_type=MESH,
        )

    def when(cond, run):
        if cond is None:
            run()
        else:
            pl.when(cond)(run)

    def send(src, dst, ssem, rsem, device, cond=None):
        when(cond, copy_of(src, dst, ssem, rsem, device).start)

    def arrived(dst, rsem, cond=None):
        when(cond, copy_of(dst, dst, 0, rsem, sibling).wait_recv)

    def sent_later(ssem, src, cond=None):
        pending.append((cond, copy_of(src, src, ssem, 0, sibling)))

    def one_send(src, dst, device):
        ssem, rsem = sends.take(1), sems.take(1)
        send(src, dst, ssem, rsem, device)
        sent_later(ssem, src)
        return rsem

    barrier = pltpu.get_barrier_semaphore()
    for dz in range(1, nz):
        pl.semaphore_signal(
            barrier, inc=1, device_id=at((z + dz) % nz, x, e), device_id_type=MESH
        )

    def greet(d, carry):
        p = (pme + d) % NE
        pl.semaphore_signal(barrier, inc=1, device_id=at(z, p % 2, p // 2), device_id_type=MESH)
        return carry

    lax.fori_loop(1, NE, greet, 0)

    DW, SM, WIN, WOUT = b["DW"], b["SM"], b["WIN"], b["WOUT"]
    UP, DN = (b["UPI"], b["UPO"]), (b["DNI"], b["DNO"])

    def fetch(src, dst):
        copy = pltpu.make_async_copy(src, dst, LS.at[locals_.take(1)])
        copy.start()
        return copy

    def columns_of_shard(k):
        shard = qkv_s if k < nq else out_s
        return shard.at[:, (k % nq) * TW : (k % nq + 1) * TW]

    own_dense = locals_.take(1)
    for k in range(nq + nb):

        @pl.when(e == k)
        def _():
            pltpu.make_async_copy(
                columns_of_shard(k), DW.at[k, z, x], LS.at[own_dense]
            ).start()

    SR = b["SR"]
    SR[z, x] = jnp.zeros((NR, RF), BF16)
    small_in = [
        fetch(gain1, b["G1"]),
        fetch(gain2, b["G2"]),
        fetch(router, b["RW"]),
    ]
    token_in = [fetch(routes, b["RR"]), fetch(xin, b["XR"]), fetch(cot, b["CR"])]
    own_in = locals_.take(1)
    for k in range(nz):
        pltpu.make_async_copy(
            ein.at[x, :, k * FC : (k + 1) * FC], WIN.at[k, z, x], LS.at[own_in]
        ).start()
    own_out = fetch(eout.at[x], WOUT.at[z, x])

    for copy in small_in:
        copy.wait()
    SR[z, x, 0:NE] = b["RW"][...]
    SR[z, x, NE : NE + 1] = b["G1"][...]
    SR[z, x, NE + 1 : NE + 2] = b["G2"][...]
    entry = lax.broadcasted_iota(jnp.int32, (NR, 128), 0)
    place = lax.broadcasted_iota(jnp.int32, (NR, 128), 1)
    pick = (
        ((entry < NE) & (entry == place))
        | ((entry >= NE) & (entry < NE + 2) & (place == entry - NE + 126))
    ).astype(BF16)
    pltpu.make_async_copy(DW.at[e, z, x], DW.at[e, z, x], LS.at[own_dense]).wait()
    pl.semaphore_wait(barrier, nz - 1 + NE - 1)

    far_first = [d for k in range(1, nz) for d in (k, nz - k) if 2 * k <= nz]
    orders = list(dict.fromkeys(far_first))
    r_dz, r_sz, s_dz, s_sz = sems.take(nz), sems.take(1), sends.take(1), sends.take(1)
    for dz in orders:
        to = at((z + dz) % nz, x, e)
        send(DW.at[e, z, x], DW.at[e, z, x], s_dz, r_dz + dz, to)
    for dz in orders:
        to = at((z + dz) % nz, x, e)
        send(SR.at[z, x], SR.at[z, x], s_sz, r_sz, to)
    sent_later(s_dz, DW.at[e, 0 : nz - 1, x])
    sent_later(s_sz, SR.at[0 : nz - 1, x])

    s_px, r_px = sends.take(1), sems.take(nz)
    s_py, r_py = sends.take(G), sems.take(G * nz)
    s_c, r_c = sends.take(1), sems.take(1)

    def spread_shard(dz):
        zz = (z + nz - dz) % nz
        piece = DW.at[e, zz, x]
        send(piece, piece, s_px, r_px + dz, across)
        for d in range(1, G):
            send(piece, piece, s_py + d, r_py + d * nz + dz, at(z, x, ((y + d) % G) * 2 + core))
        send(piece, piece, s_c, r_c, sibling)

    spread_shard(0)
    sent_later(s_px, DW.at[e, :, x])
    for d in range(1, G):
        sent_later(s_py + d, DW.at[e, :, x])
    sent_later(s_c, DW.at[0:G])

    s_xi, r_xi = sends.take(1), sems.take(1)
    for k in range(nz):
        send(ein.at[1 - x, :, k * FC : (k + 1) * FC], WIN.at[k, z, x], s_xi, r_xi, across)
    sent_later(s_xi, WIN.at[:, z, x])

    XP, CT, RT, PM = b["XP"], b["CT"], b["RT"], b["PM"]

    @pl.when(z == 0)
    def _():
        UP[0][:, 0] = jnp.zeros((nz, 2, RF, FC), BF16)
        UP[1][0] = jnp.zeros((2, CF, D), BF16)

    @pl.when(z == nz - 1)
    def _():
        DN[0][:, nz - 1] = jnp.zeros((nz, 2, RF, FC), BF16)
        DN[1][nz - 1] = jnp.zeros((2, CF, D), BF16)

    for copy in token_in:
        copy.wait()
    lane = lax.broadcasted_iota(jnp.int32, (TP, 128), 1)
    lane_f = lane.astype(F32)
    swap = (
        lax.broadcasted_iota(jnp.int32, (2, 128), 0) == lax.broadcasted_iota(jnp.int32, (2, 128), 1)
    ).astype(BF16)
    for m in range(M):
        XP[m] = jnp.zeros((TP, D), BF16)
        CT[m] = jnp.zeros((TP, D), BF16)
        RT[m] = jnp.full((TP, 128), -1.0, F32)
        XP[m, 0:T] = b["XR"][:, m, :]
        CT[m, 0:T] = b["CR"][:, m, :]
        RT[m, 0:T] = tn(b["RR"][m].astype(BF16), swap)

    def onehot(m, j):
        return RT[m][:, j : j + 1] == lane_f

    before = (
        lax.broadcasted_iota(jnp.int32, (TP, TP), 1) < lax.broadcasted_iota(jnp.int32, (TP, TP), 0)
    ).astype(BF16)
    spots = lax.broadcasted_iota(jnp.int32, (TP, S), 1).astype(F32)
    for m in range(M):
        first = onehot(m, 0).astype(F32)
        second = onehot(m, 1).astype(F32)
        rank0 = nn(before, first.astype(BF16))
        rank1 = nn(before, second.astype(BF16)) + jnp.sum(first, axis=0, keepdims=True)
        for j, (hot, rank) in enumerate(((first, rank0), (second, rank1))):
            slot = jnp.sum(hot * rank, axis=-1, keepdims=True)
            route = RT[m][:, j : j + 1]
            spot = jnp.where(route >= 0, route * CP + slot, -1.0)
            PM[m, j] = (spots == spot).astype(BF16)

    def turn_of(i):
        return 0 if i == 0 else i % (nz - 1) + 1

    groups = (range(0, 2), range(2, nz))
    s_zi = [[sends.take(1) for _ in groups] for _ in range(2)]
    s_zo = [sends.take(1) for _ in range(2)]
    r_zi = [[sems.take(nz) for _ in groups] for _ in range(2)]
    r_zo = [sems.take(2 * nz) for _ in range(2)]
    for zz in range(nz):
        for side in range(2):
            count = zz + 1 if side == 0 else nz - zz
            if count < nz:
                for g, turns in enumerate(groups):
                    sent_later(s_zi[side][g], WIN.at[0 : len(turns), 0:count], z == zz)
                sent_later(s_zo[side], WOUT.at[0:count], z == zz)

    def reach(side, d, some=None):
        begun = z - d if side == 0 else z + d
        there = (begun >= 0) if side == 0 else (begun < nz)
        last = (z == nz - 1) if side == 0 else (z == 0)
        if some is not None:
            there = there & some(begun)
        return begun, there, there & jnp.logical_not(last)

    def onward(side):
        return at((z + 1) % nz if side == 0 else (z + nz - 1) % nz, x, e)

    def pass_in(g, d, halves=(0, 1)):
        for side in range(2):
            begun, there, goes = reach(side, d)
            r = r_zi[side][g]
            if d > 0:
                arrived(WIN.at[0 : len(groups[g]), begun], r + d, there)
            if d < nz - 1:

                @pl.when(goes)
                def _():
                    for i in groups[g]:
                        k = turn_of(i) if side == 1 else nz - 1 - turn_of(i)
                        for half in halves:
                            piece = WIN.at[k, begun, x if half == 0 else 1 - x]
                            send(piece, piece, s_zi[side][g], r + d + 1, onward(side))

    def pass_out(d, half, late=None):
        xx = x if half == 0 else 1 - x
        for side in range(2):
            odd = nz - 2 if side == 0 else 1
            some = None
            if late is not None:
                some = (lambda begun: begun == odd) if late else (lambda begun: begun != odd)
            begun, there, goes = reach(side, d, some)
            r = r_zo[side] + 2 * d + half
            piece = WOUT.at[begun, xx]
            if d > 0:
                arrived(piece, r, there)
            if d < nz - 1:
                send(piece, piece, s_zo[side], r + 2, onward(side), goes)

    early, others = 0, 1
    for dz in orders:
        arrived(DW.at[e, (z + nz - dz) % nz, x], r_dz + dz)
        spread_shard(dz)
    arrived(SR.at[0 : nz - 1, x], r_sz)
    r_sx = one_send(SR.at[:, x], SR.at[:, x], across)
    pltpu.make_async_copy(WIN.at[:, z, x], WIN.at[:, z, x], LS.at[own_in]).wait()
    pass_in(early, 0, (0,))
    arrived(WIN.at[:, z, 1 - x], r_xi)
    pass_in(early, 0, (1,))
    own_out.wait()
    pass_out(0, 0)
    pass_in(others, 0)

    s_f1, r_f1 = sends.take(G), sems.take(G)
    s_f2, r_f2 = sends.take(G), sems.take(G)
    for d in range(1, G):
        sent_later(s_f1 + d, DW.at[e, 0:h, x])
        sent_later(s_f2 + d, DW.at[e, h:nz, x])

    def forward_shard(dz):
        zz = (z + nz - dz) % nz
        piece = DW.at[e, zz, 1 - x]
        arrived(piece, r_px + dz)
        for d in range(1, G):
            to = at(z, x, ((y + d) % G) * 2 + core)
            send(piece, piece, s_f1 + d, r_f1 + d, to, zz < h)
        send(piece, piece, s_c, r_c, sibling)
        for d in range(1, G):
            piece = DW.at[((y + G - d) % G) * 2 + core, zz, x]
            arrived(piece, r_py + d * nz + dz)
            send(piece, piece, s_f2 + d, r_f2 + d, across, zz >= h)
            send(piece, piece, s_c, r_c, sibling)

    for dz in [0] + orders:
        forward_shard(dz)
    for d in range(1, G):
        ee = ((y + G - d) % G) * 2 + core
        arrived(DW.at[ee, 0:h, 1 - x], r_f1 + d)
        arrived(DW.at[ee, h:nz, 1 - x], r_f2 + d)
        send(DW.at[ee, :, 1 - x], DW.at[ee, :, 1 - x], s_c, r_c, sibling)
    r_xo = one_send(eout.at[1 - x], WOUT.at[z, x], across)
    arrived(SR.at[:, 1 - x], r_sx)
    for zz in range(nz):
        for xx in range(2):
            SM[zz, xx] = tn(SR[zz, xx], pick).astype(BF16)
    arrived(DW.at[0:G], r_c)

    pass_in(early, 1)

    def dense(k):
        return DW[k].reshape(D, TW)

    small = SM[...].reshape(D, 128)
    gains = nt(pick, small)
    gain_one, gain_two = gains[NE : NE + 1], gains[NE + 1 : NE + 2]
    key_ok = lax.broadcasted_iota(jnp.int32, (1, TP), 1) < T
    low_half = lax.broadcasted_iota(jnp.int32, (1, pair), 1) < head
    N1, J, ATT, MID, N2 = b["N1"], b["J"], b["ATT"], b["MID"], b["N2"]
    GATES, XGS, XG = b["GATES"], b["XGS"], b["XG"]

    def half_of(value, i):
        keep = low_half if i == 0 else jnp.logical_not(low_half)
        return jnp.where(keep, value, jnp.zeros_like(value))

    def softmax_scores(query, keys):
        scores = jnp.where(key_ok, nt(query, keys) * scale, -1e30)
        raised = jnp.exp(scores - jnp.max(scores, axis=-1, keepdims=True))
        return raised * (1.0 / jnp.sum(raised, axis=-1, keepdims=True))

    def columns(base, hp):
        return pl.ds(pl.multiple_of(base + hp * pair, 128), pair)

    def chosen_of(m, j):
        gates = GATES[m]
        return jnp.sum(jnp.where(onehot(m, j), gates, 0.0), axis=-1, keepdims=True)

    def forward(m):
        tokens = XP[m].astype(F32)
        hat, _ = normalize(tokens)
        N1[m] = (hat * gain_one).astype(BF16)
        for k in range(nq):
            J[m, :, k * TW : (k + 1) * TW] = nn(N1[m], dense(k)).astype(BF16)

        def attend(hp, carry):
            query, keys, values = (J[m, :, columns(i * D, hp)] for i in range(3))
            total = jnp.zeros((TP, pair), F32)
            for i in range(2):
                probs = softmax_scores(half_of(query, i), keys).astype(BF16)
                total = total + nn(probs, half_of(values, i))
            ATT[m, :, columns(0, hp)] = total.astype(BF16)
            return carry

        lax.fori_loop(0, D // pair, attend, 0)
        for k in range(nb):
            cols = slice(k * TW, (k + 1) * TW)
            MID[m, :, cols] = XP[m, :, cols].astype(F32) + nn(ATT[m], dense(nq + k))
        hat, _ = normalize(MID[m])
        N2[m] = (hat * gain_two).astype(BF16)
        logits = jnp.where(lane < NE, nn(N2[m], small), -1e30)
        raised = jnp.exp(logits - jnp.max(logits, axis=-1, keepdims=True))
        GATES[m] = raised / jnp.sum(raised, axis=-1, keepdims=True)
        upstream = CT[m].astype(F32)
        XGS[m, 0] = tn(PM[m, 0] + PM[m, 1], N2[m]).astype(BF16).reshape(NE, CP, D)
        placed = tn(PM[m, 0], (chosen_of(m, 0) * upstream).astype(BF16))
        placed = placed + tn(PM[m, 1], (chosen_of(m, 1) * upstream).astype(BF16))
        XGS[m, 1] = placed.astype(BF16).reshape(NE, CP, D)

    def exchange(src, dst, m, sem):
        def one(d, carry):
            p = (pme + d) % NE
            send(src.at[m, :, p], dst.at[m, :, pme], *sem, at(z, p % 2, p // 2))
            return carry

        lax.fori_loop(1, NE, one, 0)
        sent_later(sem[0], src.at[m, :, 0 : NE - 1])
        dst[m, :, pme] = src[m, :, pme]

    def exchanged(dst, m, sem):
        arrived(dst.at[m, :, 0 : NE - 1], sem[1])

    s_go = [(sends.take(1), sems.take(1)) for _ in range(M)]
    s_back = [(sends.take(1), sems.take(1)) for _ in range(M)]
    for m in range(M):
        forward(m)
        exchange(XGS, XG, m, s_go[m])
        if m == 0:
            pass_in(early, 2) if nz <= 4 else None
    arrived(WOUT.at[z, 1 - x], r_xo)
    pass_out(0, 1, False)
    for d in range(3 if nz <= 4 else 2, nz):
        pass_in(early, d)
    pass_out(1, 0)
    pass_in(others, 1)
    pass_out(1, 1, False)
    for m in range(M):
        exchanged(XG, m, s_go[m])

    YACC, DXACC, AS, GHS = b["YACC"], b["DXACC"], b["AS"], b["GHS"]
    DWI, DWO = b["DWI"], b["DWO"]
    YACC[...] = jnp.zeros_like(YACC)
    DXACC[...] = jnp.zeros_like(DXACC)
    c0, c1 = math.sqrt(2.0 / math.pi), 0.044715

    YD, RET = b["YD"], b["RET"]
    OWN = (DWI, DWO)
    s_up = [(sends.take(1), sends.take(1)) for _ in range(2)]
    r_up = [(sems.take(nz * nz), sems.take(2 * nz)) for _ in range(2)]

    def expert_block(k, done):
        def part(m):
            tokens = XG[m, 0].reshape(S, D)
            grads = XG[m, 1].reshape(S, D)
            for xx in range(2):
                cols = slice(xx * CF, (xx + 1) * CF)
                w_in = WIN[k, :, :, :, cols].reshape(D, CF)
                w_out = WOUT[k, xx]
                hidden = nn(tokens, w_in)
                grad_acted = nt(grads, w_out)
                square = hidden * hidden
                bent = jnp.tanh(c0 * hidden * (1.0 + c1 * square))
                acted = (0.5 * hidden * (1.0 + bent)).astype(BF16)
                slope = 0.5 * (1.0 + bent) + 0.5 * c0 * hidden * (1.0 - bent * bent) * (
                    1.0 + 3.0 * c1 * square
                )
                grad_hidden = (grad_acted * slope).astype(BF16)
                AS[m, :, cols] = acted
                GHS[m, :, cols] = grad_hidden
                YACC[m] = YACC[m] + nn(acted, w_out)
                DXACC[m] = DXACC[m] + nt(grad_hidden, w_in)

        for m in range(M):
            part(m)
            if done is not None:
                done(m)
        grads = XG[:, 1].reshape(M * S, D)
        tokens = XG[:, 0].reshape(M * S, D)
        for xx in range(2):
            cols = slice(xx * CF, (xx + 1) * CF)
            DWO[k, xx] = tn(AS[:, :, cols].reshape(M * S, CF), grads).astype(BF16)
            DWI[k, :, :, :, cols] = (
                tn(tokens, GHS[:, :, cols].reshape(M * S, CF))
                .astype(BF16)
                .reshape(nz, 2, RF, CF)
            )

    def sum_step(side, i, begins):
        far = z if side == 0 else nz - 1 - z
        GOT = UP if side == 0 else DN
        turn = ((i % (nz - 1)) + 1) * jnp.minimum(i, 1)
        k = turn if side == 0 else nz - 1 - turn

        def one(j, carry):
            goal = nz - 1 - j
            t = goal if side == 0 else nz - 1 - goal
            rsem = r_up[side][0] + k * nz + t

            @pl.when(goal > far)
            def _():
                if not begins:
                    arrived(GOT[0].at[k, t], rsem)
                    DWI[k, t] = DWI[k, t] + GOT[0][k, t]
                send(DWI.at[k, t], GOT[0].at[k, t], s_up[side][0], rsem, onward(side))

            return carry

        lax.fori_loop(0, nz - 1, one, 0)

        @pl.when(turn > far)
        def _():
            for xx in (1 - x, x):
                rsem = r_up[side][1] + 2 * k + xx
                if not begins:
                    arrived(GOT[1].at[k, xx], rsem)
                    DWO[k, xx] = DWO[k, xx] + GOT[1][k, xx]
                send(DWO.at[k, xx], GOT[1].at[k, xx], s_up[side][1], rsem, onward(side))

    def sums_begin(i):
        for side in range(2):
            far = z if side == 0 else nz - 1 - z
            pl.when(far == 0)(functools.partial(sum_step, side, jnp.int32(i), True))

    def sums_pass(far_at, i):
        for side in range(2):
            far = z if side == 0 else nz - 1 - z
            pl.when(far == far_at)(functools.partial(sum_step, side, jnp.int32(i), False))

    passes = [
        (slot - i + 1, i)
        for slot in range(2 * nz - 3)
        for i in range(nz)
        if 0 < slot - i + 1 < nz - 1
    ]

    def sums_next(count):
        for _ in range(min(count, len(passes))):
            sums_pass(*passes.pop(0))

    def sums_rest():
        if len(passes) <= 2:
            return sums_next(2)

        def slot_of(slot, carry):
            for side in range(2):
                far = z if side == 0 else nz - 1 - z
                i = slot - far + 1
                ok = (far > 0) & (far < nz - 1) & (i >= 0) & (i < nz)
                pl.when(ok)(functools.partial(sum_step, side, jnp.clip(i, 0, nz - 1), False))
            return carry

        first = sum(passes[0]) - 1
        lax.fori_loop(first, 2 * nz - 3, slot_of, 0)

    for zz in range(nz):
        for side in range(2):
            count = nz - 1 - zz if side == 0 else zz
            if count > 0:
                sent_later(s_up[side][0], DWI.at[:, 0:count], z == zz)
                sent_later(s_up[side][1], DWO.at[0:count], z == zz)

    def give_back(m):
        YD[m, 0] = YACC[m].astype(BF16).reshape(NE, CP, D)
        YD[m, 1] = DXACC[m].astype(BF16).reshape(NE, CP, D)
        exchange(YD, RET, m, s_back[m])

    when_two, when_far, when_late = (1, 2, nz - 1) if nz <= 4 else (0, 0, 0)
    for i in range(nz):
        if i == when_two:
            pass_in(others, 2)
            pass_out(2, 0)
            pass_out(2, 1, False)
        if i == when_far:
            pass_out(0, 1, True)
            for d in range(3, nz):
                pass_in(others, d)
                pass_out(d, 0)
                pass_out(d, 1, False)
        if i == when_late:
            for d in range(1, nz):
                pass_out(d, 1, True)
        block = turn_of(i) + (z // h) * (nz - 1 - 2 * turn_of(i))
        expert_block(block, give_back if i == nz - 1 else None)
        sums_begin(i)

    r_fin, s_fin = (sems.take(nz), sems.take(1)), (sends.take(1), sends.take(1))
    FX, FY = (b["FXI"], b["FXO"]), (b["FYI"], b["FYO"])
    GI, GT = b["GI"], b["GT"]
    sent_later(s_fin[0], FX[0])
    sent_later(s_fin[1], FX[1])
    kept = []

    def total_of(kind, place):
        return (
            OWN[kind][place].astype(F32)
            + UP[kind][place].astype(F32)
            + DN[kind][place].astype(F32)
        )

    def sums_end_in(k):
        for side, ref, ok in ((0, UP, z > 0), (1, DN, z < nz - 1)):
            arrived(ref[0].at[k, z], r_up[side][0] + k * nz + z, ok)
        FX[0][k] = total_of(0, (k, z, 1 - x)).astype(BF16)
        send(FX[0].at[k], FY[0].at[k], s_fin[0], r_fin[0] + k, across)
        GI[x, :, k * FC : (k + 1) * FC] = total_of(0, (k, z, x))

    def sums_end_out():
        for xx, mine in ((1 - x, False), (x, True)):
            for side, ref, ok in ((0, UP, z > 0), (1, DN, z < nz - 1)):
                arrived(ref[1].at[z, xx], r_up[side][1] + 2 * z + xx, ok)
            if mine:
                GT[x] = total_of(1, (z, xx))
            else:
                FX[1][...] = total_of(1, (z, xx)).astype(BF16)
                send(FX[1], FY[1], s_fin[1], r_fin[1], across)

    def sums_close():
        kept.append(fetch(GI.at[x], gein.at[x]))
        kept.append(fetch(GT.at[x], geout.at[x]))
        for k in range(nz):
            arrived(FY[0].at[k], r_fin[0] + k)
            GI[1 - x, :, k * FC : (k + 1) * FC] = FY[0][k].astype(F32)
        kept.append(fetch(GI.at[1 - x], gein.at[1 - x]))
        arrived(FY[1], r_fin[1])
        GT[1 - x] = FY[1][...].astype(F32)
        kept.append(fetch(GT.at[1 - x], geout.at[1 - x]))

    GM, GA, GJ, GR = b["GM"], b["GA"], b["GJ"], b["GR"]
    DG = b["DG"]
    GR[...] = jnp.zeros_like(GR)

    def backward_top(m):
        result = RET[m, 0].reshape(S, D)
        picked0 = nn(PM[m, 0], result)
        picked1 = nn(PM[m, 1], result)
        out = MID[m] + chosen_of(m, 0) * picked0 + chosen_of(m, 1) * picked1
        b["AR"][:, m, :] = out[0:T]
        upstream = CT[m].astype(F32)
        gates = GATES[m]
        grad_gates = jnp.where(
            onehot(m, 0), jnp.sum(upstream * picked0, axis=-1, keepdims=True), 0.0
        ) + jnp.where(onehot(m, 1), jnp.sum(upstream * picked1, axis=-1, keepdims=True), 0.0)
        grad_logits = (
            gates * (grad_gates - jnp.sum(grad_gates * gates, axis=-1, keepdims=True))
        ).astype(BF16)
        GR[0:NE] = GR[0:NE] + tn(grad_logits, N2[m])[0:NE]
        grad = nn(PM[m, 0] + PM[m, 1], RET[m, 1].reshape(S, D)) + nt(grad_logits, small)
        hat, rstd = normalize(MID[m])
        GR[NE + 1 : NE + 2] = GR[NE + 1 : NE + 2] + jnp.sum(grad * hat, axis=0, keepdims=True)
        grad_middle = upstream + normalize_back(grad * gain_two, hat, rstd)
        GM[m] = grad_middle
        branch = grad_middle.astype(BF16)
        N2[m] = branch
        back = None
        for k in range(nb):
            term = nt(branch[:, k * TW : (k + 1) * TW], dense(nq + k))
            back = term if back is None else back + term
        GA[m] = back.astype(BF16)

    def backward_heads(m):
        def attend(hp, carry):
            query, keys, values = (J[m, :, columns(i * D, hp)] for i in range(3))
            grads = GA[m, :, columns(0, hp)]
            grad_query = jnp.zeros((TP, pair), F32)
            grad_keys = jnp.zeros((TP, pair), F32)
            grad_values = jnp.zeros((TP, pair), F32)
            for i in range(2):
                part = half_of(query, i)
                upstream = half_of(grads, i)
                probs = softmax_scores(part, keys)
                grad_probs = nt(upstream, values)
                grad_values = grad_values + tn(probs.astype(BF16), upstream)
                grad_scores = (
                    probs
                    * (grad_probs - jnp.sum(grad_probs * probs, axis=-1, keepdims=True))
                ).astype(BF16)
                grad_query = grad_query + nn(grad_scores, half_of(keys, i))
                grad_keys = grad_keys + tn(grad_scores, part)
            GJ[m, :, columns(0, hp)] = (grad_query * scale).astype(BF16)
            GJ[m, :, columns(D, hp)] = (grad_keys * scale).astype(BF16)
            GJ[m, :, columns(2 * D, hp)] = grad_values.astype(BF16)
            return carry

        lax.fori_loop(0, D // pair, attend, 0)

    def backward_end(m):
        grad = None
        for k in range(nq):
            term = nt(GJ[m, :, k * TW : (k + 1) * TW], dense(k))
            grad = term if grad is None else grad + term
        hat, rstd = normalize(XP[m].astype(F32))
        GR[NE : NE + 1] = GR[NE : NE + 1] + jnp.sum(grad * hat, axis=0, keepdims=True)
        full = GM[m] + normalize_back(grad * gain_one, hat, rstd)
        b["IG"][m, :, 0, :] = full[0:T]

    sums_next(1)
    for m in range(M):
        exchanged(RET, m, s_back[m])
        backward_top(m)
        backward_heads(m)
        sums_next(2)
    for k in range(nb):
        part = tn(
            ATT[...].reshape(M * TP, D), N2[:, :, k * TW : (k + 1) * TW].reshape(M * TP, TW)
        )
        DG[nq + k] = part.astype(BF16).reshape(nz, 2, RF, TW)
    for k in range(nq):
        part = tn(
            N1[...].reshape(M * TP, D), GJ[:, :, k * TW : (k + 1) * TW].reshape(M * TP, TW)
        )
        DG[k] = part.astype(BF16).reshape(nz, 2, RF, TW)
    RB1, RY1, RX1, RX2, RY2, RZ, FIN = (
        b[k] for k in ("RB1", "RY1", "RX1", "RX2", "RY2", "RZ", "FIN")
    )
    GB, SB1, SB2, SB3, SB4 = (b[k] for k in ("GB", "SB1", "SB2", "SB3", "SB4"))
    s_r1, r_r1 = sends.take(1), sems.take(1)
    for j in range(G):
        send(DG.at[2 * j + 1 - core], RB1.at[j], s_r1, r_r1, sibling)
    sent_later(s_r1, RB1)
    for m in range(M):
        backward_end(m)
    b["AO"][...] = b["AR"][...].astype(BF16)
    kept.append(fetch(b["AO"], act))
    kept.append(fetch(b["IG"], igrad))
    GB[...] = GR[...].astype(BF16)
    r_b1 = one_send(GB, SB1, sibling)
    arrived(RB1, r_r1)
    for j in range(G):
        DG[2 * j + core] = DG[2 * j + core] + RB1[j]
    s_ry1, r_ry1 = sends.take(G), sems.take(G)
    for d in range(1, G):
        q = (y + d) % G
        piece = DG.at[2 * q + core, 0:h]
        send(piece, RY1.at[y], s_ry1 + d, r_ry1 + d, at(z, x, 2 * q + core))
        sent_later(s_ry1 + d, piece)
    s_rx1, r_rx1 = sends.take(1), sems.take(1)
    for j in range(G):
        send(DG.at[2 * j + core, h:nz, 1 - x], RX1.at[j], s_rx1, r_rx1, across)
    sent_later(s_rx1, RX1)
    arrived(SB1, r_b1)
    SB2[y] = GB[...] + SB1[...]
    s_b2, r_b2 = sends.take(G), sems.take(G)
    for d in range(1, G):
        send(SB2.at[y], SB2.at[y], s_b2 + d, r_b2 + d, at(z, x, ((y + d) % G) * 2 + core))
        sent_later(s_b2 + d, SB2.at[y])
    sums_next(1)
    for d in range(1, G):
        q = (y + G - d) % G
        arrived(RY1.at[q], r_ry1 + d)
        DG[e, 0:h] = DG[e, 0:h] + RY1[q]
    r_rx2 = one_send(DG.at[e, 0:h, 1 - x], RX2, across)
    arrived(RX1, r_rx1)
    for j in range(G):
        DG[2 * j + core, h:nz, x] = DG[2 * j + core, h:nz, x] + RX1[j]
    s_ry2, r_ry2 = sends.take(G), sems.take(G)
    for d in range(1, G):
        q = (y + d) % G
        piece = DG.at[2 * q + core, h:nz, x]
        send(piece, RY2.at[y], s_ry2 + d, r_ry2 + d, at(z, x, 2 * q + core))
        sent_later(s_ry2 + d, piece)
    for d in range(1, G):
        arrived(SB2.at[(y + G - d) % G], r_b2 + d)
    total = SB2[0].astype(F32)
    for j in range(1, G):
        total = total + SB2[j].astype(F32)
    SB3[x] = total.astype(BF16)
    r_b3 = one_send(SB3.at[x], SB3.at[x], across)
    sums_next(1)
    arrived(RX2, r_rx2)
    DG[e, 0:h, x] = DG[e, 0:h, x] + RX2[...]
    for d in range(1, G):
        q = (y + G - d) % G
        arrived(RY2.at[q], r_ry2 + d)
        DG[e, h:nz, x] = DG[e, h:nz, x] + RY2[q]
    s_rz, r_rz = sends.take(1), sems.take(1)
    for dz in orders:
        zz = (z + dz) % nz
        send(DG.at[e, zz, x], RZ.at[z], s_rz, r_rz, at(zz, x, e))
    sent_later(s_rz, RZ.at[0 : nz - 1])
    arrived(SB3.at[1 - x], r_b3)
    SB4[z] = SB3[0] + SB3[1]
    s_b4, r_b4 = sends.take(1), sems.take(1)
    for dz in orders:
        send(SB4.at[z], SB4.at[z], s_b4, r_b4, at((z + dz) % nz, x, e))
    sent_later(s_b4, SB4.at[0 : nz - 1])
    sums_rest()
    ends = [0, nz - 1] + list(range(1, nz - 1))
    for k in ends[:2]:
        sums_end_in(k)
    RZ[z] = DG[e, z, x]
    arrived(RZ.at[0 : nz - 1], r_rz)
    total = RZ[0].astype(F32)
    for k in range(1, nz):
        total = total + RZ[k].astype(F32)
    FIN[e] = total.astype(BF16)
    s_fe, r_fe = sends.take(1), sems.take(1)

    def hand_out(d, carry):
        send(FIN.at[e], FIN.at[e], s_fe, r_fe, at(z, x, (e + d) % E))
        return carry

    lax.fori_loop(1, E, hand_out, 0)
    sent_later(s_fe, FIN.at[0 : E - 1])
    arrived(SB4.at[0 : nz - 1], r_b4)
    total = SB4[0].astype(F32)
    for k in range(1, nz):
        total = total + SB4[k].astype(F32)
    mine = (
        lax.broadcasted_iota(jnp.int32, (D, RF), 0)
        == lax.broadcasted_iota(jnp.int32, (D, RF), 1) + f * RF
    ).astype(F32)
    b["GS"][...] = lax.dot_general(
        total,
        mine,
        (((1,), (0,)), ((), ())),
        precision=lax.Precision.HIGHEST,
        preferred_element_type=F32,
    )
    kept.append(fetch(b["GS"].at[0:NE], grouter))
    kept.append(fetch(b["GS"].at[NE : NE + 1], ggain1))
    kept.append(fetch(b["GS"].at[NE + 1 : NE + 2], ggain2))
    sums_end_out()
    for k in ends[2:]:
        sums_end_in(k)
    sums_close()
    arrived(FIN.at[0 : E - 1], r_fe)
    for k in range(nq):
        b["GQ"][:, k * TW : (k + 1) * TW] = FIN[k].astype(F32)
    for k in range(nb):
        b["GO"][:, k * TW : (k + 1) * TW] = FIN[nq + k].astype(F32)
    kept.append(fetch(b["GQ"], gqkv))
    kept.append(fetch(b["GO"], gout))

    for cond, copy in pending:
        when(cond, copy.wait_send)
    for copy in kept:
        copy.wait()
    used = (sends.used, sems.used, locals_.used)
    assert all(a <= b for a, b in zip(used, counts)), (used, counts)


def hand_over(*refs):
    source, target, held = refs[:9], refs[9:18], refs[18:27]
    sem = refs[27]
    order = sorted(range(9), key=lambda k: -math.prod(source[k].shape))
    into = {k: pltpu.make_async_copy(source[k], held[k], sem.at[0, k]) for k in order}
    out = {k: pltpu.make_async_copy(held[k], target[k], sem.at[1, k]) for k in order}
    for k in order:
        into[k].start()
    for k in order:
        into[k].wait()
        out[k].start()
    for k in order:
        out[k].wait()


def body(
    mesh_shape,
    inputs,
    gain_attn,
    qkv_weight,
    out_weight,
    gain_moe,
    router_weight,
    expert_in,
    expert_out,
    routes,
    cotangent,
):
    micro, images, seq, width = inputs.shape
    c = layout(mesh_shape, micro, images * seq, width, expert_in.shape[2])
    rows = images * seq
    scratch = scratch_of(c)
    names = list(scratch)
    nz, G = c["nz"], c["G"]
    counts = (31 + 6 * G, 14 + 16 * nz + 2 * nz * nz + G * nz + 5 * G, 20)
    shapes = (
        ((rows, micro, width), BF16),
        ((micro, rows, 1, width), F32),
        (qkv_weight.shape, F32),
        (out_weight.shape, F32),
        ((1, c["RF"]), F32),
        ((1, c["RF"]), F32),
        ((c["NE"], c["RF"]), F32),
        (expert_in.shape, F32),
        (expert_out.shape, F32),
    )
    shapes = [jax.ShapeDtypeStruct(s, t) for s, t in shapes]
    anywhere = pl.BlockSpec(memory_space=pltpu.HBM)
    results = pl.pallas_call(
        functools.partial(kernel, c, names, counts),
        out_shape=shapes,
        in_specs=[anywhere] * 10,
        out_specs=[anywhere] * 9,
        scratch_shapes=[pltpu.VMEM(s, t) for s, t in scratch.values()]
        + [pltpu.SemaphoreType.DMA((count,)) for count in counts],
        compiler_params=pltpu.CompilerParams(
            collective_id=0, has_side_effects=True, vmem_limit_bytes=60 * 1024 * 1024
        ),
    )(
        jnp.transpose(inputs, (1, 2, 0, 3)).reshape(rows, micro, width),
        jnp.transpose(cotangent, (1, 2, 0, 3)).reshape(rows, micro, width),
        jnp.transpose(routes, (0, 1, 3, 2)).reshape(micro, 2, rows),
        qkv_weight,
        out_weight,
        gain_attn[None, :],
        gain_moe[None, :],
        router_weight.T,
        expert_in,
        expert_out,
    )
    act, igrad, gqkv, gout, ggain1, ggain2, grouter, gein, geout = pl.pallas_call(
        hand_over,
        out_shape=shapes,
        in_specs=[anywhere] * 9,
        out_specs=[anywhere] * 9,
        scratch_shapes=[pltpu.VMEM(s.shape, s.dtype) for s in shapes]
        + [pltpu.SemaphoreType.DMA((2, 9))],
        compiler_params=pltpu.CompilerParams(vmem_limit_bytes=60 * 1024 * 1024),
    )(*results)
    return (
        jnp.transpose(act.reshape(images, seq, micro, width), (2, 0, 1, 3)),
        igrad.reshape(inputs.shape),
        ggain1[0],
        gqkv,
        gout,
        ggain2[0],
        grouter.T,
        gein,
        geout,
    )


def solution(mesh):
    return jax.shard_map(
        functools.partial(body, dict(mesh.shape)),
        mesh=mesh,
        in_specs=(
            P(None, ("fsdp", "expert"), None, None),
            P("fsdp"),
            P("fsdp", None),
            P("fsdp", None),
            P("fsdp"),
            P("fsdp", None),
            P("expert", "fsdp", None),
            P("expert", "fsdp", None),
            P(None, ("fsdp", "expert"), None, None),
            P(None, ("fsdp", "expert"), None, None),
        ),
        out_specs=(
            P(None, ("fsdp", "expert"), None, None),
            P(None, ("fsdp", "expert"), None, None),
            P("fsdp"),
            P("fsdp", None),
            P("fsdp", None),
            P("fsdp"),
            P("fsdp", None),
            P("expert", "fsdp", None),
            P("expert", "fsdp", None),
        ),
        check_vma=False,
    )
```

time: 209 us -> 158 us (0.76)
  Pallas kernels: 193 us -> 157 us
  local copies, waits for them, and re-layouts: 14.5 us -> 0 us
    pallas_call x1 -> x2, Pallas kernels: 193 us -> 157 us  [the longest x1 154 us: body(): pl.pallas_call(functools.partial(kernel, c, names, counts), out_shape=sha...]
    unnamed x29 -> x0, local copies, waits for them, and re-layouts: 11.4 us -> none
    reshape x1 -> x0, local copies, waits for them, and re-layouts: 2.09 us -> none  [body(): cotangent.reshape(micro, rows, width)]
where the time goes in v2:
time: 158 us
  Pallas kernels  157 us (99%)
    pallas_call x1, Pallas kernels, body(): pl.pallas_call(functools.partial(kernel, c, names, counts), out_shape=sha...  154 us
    pallas_call x1, Pallas kernels, body(): pl.pallas_call(hand_over, out_shape=shapes, in_specs=[anywhere] * 9, out_...  3.27 us

profile of v2, /device:TPU:0, one launch (start us, length us, event | category | flops | bytes accessed | tf_op | source)
XLA Modules:
  0.0 158.0 jit_solution(321227167575064728)
XLA Ops:
  0.6 153.9 %shard_map.169 = (bf16[197,2,512]{2,1,0:T(2,128)(2,1)}, f32[2,197,1,512]{3,2,1,0:T(1,128)}, f32[64,1536]{1,0:T(8,128)}, f32[64,512]{1,0:T(8,128)}, f32[1,64]{1,0...) custom-call(bf16[197,2,512]{2,1,0:T(2,128)(2,1)} %bitcast.21, ...), custom_call_target="tpu_custom_call" | custom-call | tf_op jit(solution)/shard_map/pallas_call | solution.py:1000
  154.5 3.3 %shard_map.170 = (bf16[197,2,512]{2,1,0:T(2,128)(2,1)}, f32[2,197,1,512]{3,2,1,0:T(1,128)}, f32[64,1536]{1,0:T(8,128)}, f32[64,512]{1,0:T(8,128)}, f32[1,64]{1,0...) custom-call(bf16[197,2,512]{2,1,0:T(2,128)(2,1)} %get-tuple-element.27.refs_0_, ...), custom_call_target="tpu_custom_call" | custom-call | tf_op jit(solution)/shard_map/pallas_call | solution.py:1022

commit v3 on v2

--- a/solution.py
+++ b/solution.py
@@ -111,10 +111,20 @@
         "N2": ((M, TP, D), BF16),
         "GATES": ((M, TP, 128), F32),
         "PM": ((M, 2, TP, S), BF16),
-        "XGS": ((M, 2, NE, CP, D), BF16),
-        "XG": ((M, 2, NE, CP, D), BF16),
-        "YD": ((M, 2, NE, CP, D), BF16),
-        "RET": ((M, 2, NE, CP, D), BF16),
+        "XS": ((M, NE, CP, D), BF16),
+        "XB": ((M, NE, CP, D), BF16),
+        "GSS": ((M, NE, CP, D), BF16),
+        "GRB": ((M, NE, CP, D), BF16),
+        "CSS": ((M, NE, 8, 128), F32),
+        "CSB": ((M, NE, 8, 128), F32),
+        "CROW": ((8, S), F32),
+        "GC": ((M, S, D), BF16),
+        "YS": ((M, NE, CP, D), BF16),
+        "YB": ((M, NE, CP, D), BF16),
+        "DXS": ((M, NE, CP, D), BF16),
+        "DXB": ((M, NE, CP, D), BF16),
+        "GCS": ((M, NE, 8, 128), F32),
+        "GCB": ((M, NE, 8, 128), F32),
         "YACC": ((M, S, D), F32),
         "DXACC": ((M, S, D), F32),
         "AS": ((M, S, FC), BF16),
@@ -394,13 +404,17 @@
                             piece = WIN.at[k, begun, x if half == 0 else 1 - x]
                             send(piece, piece, s_zi[side][g], r + d + 1, onward(side))
 
-    def pass_out(d, half, late=None):
+    def pass_out(d, half, late=None, near=None):
         xx = x if half == 0 else 1 - x
         for side in range(2):
             odd = nz - 2 if side == 0 else 1
             some = None
             if late is not None:
                 some = (lambda begun: begun == odd) if late else (lambda begun: begun != odd)
+            if near is not None:
+                lower = (z < h) if side == 0 else (z >= h)
+                chosen = lower if near else jnp.logical_not(lower)
+                some = lambda begun, odd=odd, chosen=chosen: (begun != odd) & chosen
             begun, there, goes = reach(side, d, some)
             r = r_zo[side] + 2 * d + half
             piece = WOUT.at[begun, xx]
@@ -410,18 +424,20 @@
                 send(piece, piece, s_zo[side], r + 2, onward(side), goes)
 
     early, others = 0, 1
-    for dz in orders:
+    for dz in orders[:2]:
+        arrived(DW.at[e, (z + nz - dz) % nz, x], r_dz + dz)
+        spread_shard(dz)
+    pltpu.make_async_copy(WIN.at[:, z, x], WIN.at[:, z, x], LS.at[own_in]).wait()
+    pass_in(early, 0, (0,))
+    for dz in orders[2:]:
         arrived(DW.at[e, (z + nz - dz) % nz, x], r_dz + dz)
         spread_shard(dz)
     arrived(SR.at[0 : nz - 1, x], r_sz)
     r_sx = one_send(SR.at[:, x], SR.at[:, x], across)
-    pltpu.make_async_copy(WIN.at[:, z, x], WIN.at[:, z, x], LS.at[own_in]).wait()
-    pass_in(early, 0, (0,))
     arrived(WIN.at[:, z, 1 - x], r_xi)
     pass_in(early, 0, (1,))
     own_out.wait()
     pass_out(0, 0)
-    pass_in(others, 0)
 
     s_f1, r_f1 = sends.take(G), sems.take(G)
     s_f2, r_f2 = sends.take(G), sems.take(G)
@@ -458,6 +474,7 @@
     arrived(DW.at[0:G], r_c)
 
     pass_in(early, 1)
+    pass_in(others, 0)
 
     def dense(k):
         return DW[k].reshape(D, TW)
@@ -468,7 +485,9 @@
     key_ok = lax.broadcasted_iota(jnp.int32, (1, TP), 1) < T
     low_half = lax.broadcasted_iota(jnp.int32, (1, pair), 1) < head
     N1, J, ATT, MID, N2 = b["N1"], b["J"], b["ATT"], b["MID"], b["N2"]
-    GATES, XGS, XG = b["GATES"], b["XGS"], b["XG"]
+    GATES, XS, XB, GC, CROW = (b[k] for k in ("GATES", "XS", "XB", "GC", "CROW"))
+    GSS, GRB, CSS, CSB = (b[k] for k in ("GSS", "GRB", "CSS", "CSB"))
+    GCS, GCB, YS, YB, DXS, DXB = (b[k] for k in ("GCS", "GCB", "YS", "YB", "DXS", "DXB"))
 
     def half_of(value, i):
         keep = low_half if i == 0 else jnp.logical_not(low_half)
@@ -511,41 +530,56 @@
         logits = jnp.where(lane < NE, nn(N2[m], small), -1e30)
         raised = jnp.exp(logits - jnp.max(logits, axis=-1, keepdims=True))
         GATES[m] = raised / jnp.sum(raised, axis=-1, keepdims=True)
-        upstream = CT[m].astype(F32)
-        XGS[m, 0] = tn(PM[m, 0] + PM[m, 1], N2[m]).astype(BF16).reshape(NE, CP, D)
-        placed = tn(PM[m, 0], (chosen_of(m, 0) * upstream).astype(BF16))
-        placed = placed + tn(PM[m, 1], (chosen_of(m, 1) * upstream).astype(BF16))
-        XGS[m, 1] = placed.astype(BF16).reshape(NE, CP, D)
+        XS[m] = tn(PM[m, 0] + PM[m, 1], N2[m]).astype(BF16).reshape(NE, CP, D)
+        weight = PM[m, 0].astype(F32) * chosen_of(m, 0) + PM[m, 1].astype(F32) * chosen_of(m, 1)
+        CROW[0:1] = jnp.sum(weight, axis=0, keepdims=True)
+        for k in range(NE):
+            CSS[m, k, 0:1, 0:CP] = CROW[0:1, k * CP : (k + 1) * CP]
+
+    diagonal = lax.broadcasted_iota(jnp.int32, (CP, 128), 0) == lax.broadcasted_iota(
+        jnp.int32, (CP, 128), 1
+    )
+
+    def scale_grads(m):
+        for p in range(NE):
+            by_lane = CSB[m, p, 0:1]
+            weight = jnp.sum(jnp.where(diagonal, by_lane, 0.0), axis=1, keepdims=True)
+            GC[m, p * CP : (p + 1) * CP] = (weight * GRB[m, p].astype(F32)).astype(BF16)
 
     def exchange(src, dst, m, sem):
         def one(d, carry):
             p = (pme + d) % NE
-            send(src.at[m, :, p], dst.at[m, :, pme], *sem, at(z, p % 2, p // 2))
+            send(src.at[m, p], dst.at[m, pme], *sem, at(z, p % 2, p // 2))
             return carry
 
         lax.fori_loop(1, NE, one, 0)
-        sent_later(sem[0], src.at[m, :, 0 : NE - 1])
-        dst[m, :, pme] = src[m, :, pme]
+        sent_later(sem[0], src.at[m, 0 : NE - 1])
+        dst[m, pme] = src[m, pme]
 
     def exchanged(dst, m, sem):
-        arrived(dst.at[m, :, 0 : NE - 1], sem[1])
-
-    s_go = [(sends.take(1), sems.take(1)) for _ in range(M)]
-    s_back = [(sends.take(1), sems.take(1)) for _ in range(M)]
+        arrived(dst.at[m, 0 : NE - 1], sem[1])
+
+    def pairs():
+        return [(sends.take(1), sems.take(1)) for _ in range(M)]
+
+    s_x, s_cs, s_gr, s_dx, s_gc, s_y = (pairs() for _ in range(6))
+    for m in range(M):
+        GSS[m] = tn(PM[m, 0] + PM[m, 1], CT[m]).astype(BF16).reshape(NE, CP, D)
+        exchange(GSS, GRB, m, s_gr[m])
     for m in range(M):
         forward(m)
-        exchange(XGS, XG, m, s_go[m])
+        exchange(XS, XB, m, s_x[m])
+        exchange(CSS, CSB, m, s_cs[m])
         if m == 0:
-            pass_in(early, 2) if nz <= 4 else None
-    arrived(WOUT.at[z, 1 - x], r_xo)
-    pass_out(0, 1, False)
-    for d in range(3 if nz <= 4 else 2, nz):
+            arrived(WOUT.at[z, 1 - x], r_xo)
+            pass_out(0, 1, False)
+    for d in range(2, nz):
         pass_in(early, d)
     pass_out(1, 0)
     pass_in(others, 1)
-    pass_out(1, 1, False)
-    for m in range(M):
-        exchanged(XG, m, s_go[m])
+    pass_out(1, 1, False, True)
+    if nz > 4:
+        pass_out(1, 1, False, False)
 
     YACC, DXACC, AS, GHS = b["YACC"], b["DXACC"], b["AS"], b["GHS"]
     DWI, DWO = b["DWI"], b["DWO"]
@@ -553,39 +587,34 @@
     DXACC[...] = jnp.zeros_like(DXACC)
     c0, c1 = math.sqrt(2.0 / math.pi), 0.044715
 
-    YD, RET = b["YD"], b["RET"]
     OWN = (DWI, DWO)
     s_up = [(sends.take(1), sends.take(1)) for _ in range(2)]
     r_up = [(sems.take(nz * nz), sems.take(2 * nz)) for _ in range(2)]
 
-    def expert_block(k, done):
-        def part(m):
-            tokens = XG[m, 0].reshape(S, D)
-            grads = XG[m, 1].reshape(S, D)
-            for xx in range(2):
-                cols = slice(xx * CF, (xx + 1) * CF)
-                w_in = WIN[k, :, :, :, cols].reshape(D, CF)
-                w_out = WOUT[k, xx]
-                hidden = nn(tokens, w_in)
-                grad_acted = nt(grads, w_out)
-                square = hidden * hidden
-                bent = jnp.tanh(c0 * hidden * (1.0 + c1 * square))
-                acted = (0.5 * hidden * (1.0 + bent)).astype(BF16)
-                slope = 0.5 * (1.0 + bent) + 0.5 * c0 * hidden * (1.0 - bent * bent) * (
-                    1.0 + 3.0 * c1 * square
-                )
-                grad_hidden = (grad_acted * slope).astype(BF16)
-                AS[m, :, cols] = acted
-                GHS[m, :, cols] = grad_hidden
-                YACC[m] = YACC[m] + nn(acted, w_out)
-                DXACC[m] = DXACC[m] + nt(grad_hidden, w_in)
-
-        for m in range(M):
-            part(m)
-            if done is not None:
-                done(m)
-        grads = XG[:, 1].reshape(M * S, D)
-        tokens = XG[:, 0].reshape(M * S, D)
+    def expert_part(k, m):
+        tokens = XB[m].reshape(S, D)
+        grads = GC[m]
+        for xx in range(2):
+            cols = slice(xx * CF, (xx + 1) * CF)
+            w_in = WIN[k, :, :, :, cols].reshape(D, CF)
+            w_out = WOUT[k, xx]
+            hidden = nn(tokens, w_in)
+            grad_acted = nt(grads, w_out)
+            square = hidden * hidden
+            bent = jnp.tanh(c0 * hidden * (1.0 + c1 * square))
+            acted = (0.5 * hidden * (1.0 + bent)).astype(BF16)
+            slope = 0.5 * (1.0 + bent) + 0.5 * c0 * hidden * (1.0 - bent * bent) * (
+                1.0 + 3.0 * c1 * square
+            )
+            grad_hidden = (grad_acted * slope).astype(BF16)
+            AS[m, :, cols] = acted
+            GHS[m, :, cols] = grad_hidden
+            YACC[m] = YACC[m] + nn(acted, w_out)
+            DXACC[m] = DXACC[m] + nt(grad_hidden, w_in)
+
+    def expert_weights(k):
+        grads = GC[...].reshape(M * S, D)
+        tokens = XB[...].reshape(M * S, D)
         for xx in range(2):
             cols = slice(xx * CF, (xx + 1) * CF)
             DWO[k, xx] = tn(AS[:, :, cols].reshape(M * S, CF), grads).astype(BF16)
@@ -601,7 +630,7 @@
         turn = ((i % (nz - 1)) + 1) * jnp.minimum(i, 1)
         k = turn if side == 0 else nz - 1 - turn
 
-        def one(j, carry):
+        def tokens_side(j, carry):
             goal = nz - 1 - j
             t = goal if side == 0 else nz - 1 - goal
             rsem = r_up[side][0] + k * nz + t
@@ -615,10 +644,7 @@
 
             return carry
 
-        lax.fori_loop(0, nz - 1, one, 0)
-
-        @pl.when(turn > far)
-        def _():
+        def results_side():
             for xx in (1 - x, x):
                 rsem = r_up[side][1] + 2 * k + xx
                 if not begins:
@@ -626,6 +652,10 @@
                     DWO[k, xx] = DWO[k, xx] + GOT[1][k, xx]
                 send(DWO.at[k, xx], GOT[1].at[k, xx], s_up[side][1], rsem, onward(side))
 
+        pl.when(turn == nz - 1)(results_side)
+        lax.fori_loop(0, nz - 1, tokens_side, 0)
+        pl.when((turn > far) & (turn < nz - 1))(results_side)
+
     def sums_begin(i):
         for side in range(2):
             far = z if side == 0 else nz - 1 - z
@@ -636,31 +666,27 @@
             far = z if side == 0 else nz - 1 - z
             pl.when(far == far_at)(functools.partial(sum_step, side, jnp.int32(i), False))
 
-    passes = [
-        (slot - i + 1, i)
-        for slot in range(2 * nz - 3)
-        for i in range(nz)
-        if 0 < slot - i + 1 < nz - 1
-    ]
-
-    def sums_next(count):
-        for _ in range(min(count, len(passes))):
-            sums_pass(*passes.pop(0))
+    passes = [(far, i) for far in range(1, nz - 1) for i in range(nz)]
+
+    def sums_now(*wanted):
+        for far, i in wanted:
+            if (far, i) in passes:
+                passes.remove((far, i))
+                sums_pass(far, i)
 
     def sums_rest():
-        if len(passes) <= 2:
-            return sums_next(2)
-
-        def slot_of(slot, carry):
-            for side in range(2):
-                far = z if side == 0 else nz - 1 - z
-                i = slot - far + 1
-                ok = (far > 0) & (far < nz - 1) & (i >= 0) & (i < nz)
-                pl.when(ok)(functools.partial(sum_step, side, jnp.clip(i, 0, nz - 1), False))
-            return carry
-
-        first = sum(passes[0]) - 1
-        lax.fori_loop(first, 2 * nz - 3, slot_of, 0)
+        for far in range(1, nz - 1):
+            left = [i for k, i in passes if k == far]
+            if len(left) <= 1:
+                for i in left:
+                    sums_pass(far, i)
+            else:
+
+                def one(i, carry, far=far):
+                    sums_pass(far, i)
+                    return carry
+
+                lax.fori_loop(left[0], nz, one, 0)
 
     for zz in range(nz):
         for side in range(2):
@@ -670,9 +696,17 @@
                 sent_later(s_up[side][1], DWO.at[0:count], z == zz)
 
     def give_back(m):
-        YD[m, 0] = YACC[m].astype(BF16).reshape(NE, CP, D)
-        YD[m, 1] = DXACC[m].astype(BF16).reshape(NE, CP, D)
-        exchange(YD, RET, m, s_back[m])
+        DXS[m] = DXACC[m].astype(BF16).reshape(NE, CP, D)
+        exchange(DXS, DXB, m, s_dx[m])
+        results = YACC[m].astype(BF16)
+        YS[m] = results.reshape(NE, CP, D)
+        for p in range(NE):
+            rows = slice(p * CP, (p + 1) * CP)
+            weight = jnp.sum(
+                results[rows].astype(F32) * GRB[m, p].astype(F32), axis=1, keepdims=True
+            )
+            GCS[m, p, 0:1] = jnp.sum(jnp.where(diagonal, weight, 0.0), axis=0, keepdims=True)
+        exchange(GCS, GCB, m, s_gc[m])
 
     when_two, when_far, when_late = (1, 2, nz - 1) if nz <= 4 else (0, 0, 0)
     for i in range(nz):
@@ -690,7 +724,18 @@
             for d in range(1, nz):
                 pass_out(d, 1, True)
         block = turn_of(i) + (z // h) * (nz - 1 - 2 * turn_of(i))
-        expert_block(block, give_back if i == nz - 1 else None)
+        for m in range(M):
+            if i == 0:
+                exchanged(GRB, m, s_gr[m])
+                exchanged(XB, m, s_x[m])
+                exchanged(CSB, m, s_cs[m])
+                scale_grads(m)
+            expert_part(block, m)
+            if i == 0 and m == 0 and nz <= 4:
+                pass_out(1, 1, False, False)
+            if i == nz - 1:
+                give_back(m)
+        expert_weights(block)
         sums_begin(i)
 
     r_fin, s_fin = (sems.take(nz), sems.take(1)), (sends.take(1), sends.take(1))
@@ -739,22 +784,28 @@
     DG = b["DG"]
     GR[...] = jnp.zeros_like(GR)
 
+    def outputs(m):
+        results = YB[m].reshape(S, D)
+        out = MID[m] + chosen_of(m, 0) * nn(PM[m, 0], results)
+        b["AR"][:, m, :] = (out + chosen_of(m, 1) * nn(PM[m, 1], results))[0:T]
+
     def backward_top(m):
-        result = RET[m, 0].reshape(S, D)
-        picked0 = nn(PM[m, 0], result)
-        picked1 = nn(PM[m, 1], result)
-        out = MID[m] + chosen_of(m, 0) * picked0 + chosen_of(m, 1) * picked1
-        b["AR"][:, m, :] = out[0:T]
         upstream = CT[m].astype(F32)
+        for k in range(NE):
+            CROW[0:1, k * CP : (k + 1) * CP] = GCB[m, k, 0:1, 0:CP]
+
+        def grad_chosen(j):
+            return jnp.sum(PM[m, j].astype(F32) * CROW[0:1], axis=-1, keepdims=True)
+
         gates = GATES[m]
-        grad_gates = jnp.where(
-            onehot(m, 0), jnp.sum(upstream * picked0, axis=-1, keepdims=True), 0.0
-        ) + jnp.where(onehot(m, 1), jnp.sum(upstream * picked1, axis=-1, keepdims=True), 0.0)
+        grad_gates = jnp.where(onehot(m, 0), grad_chosen(0), 0.0) + jnp.where(
+            onehot(m, 1), grad_chosen(1), 0.0
+        )
         grad_logits = (
             gates * (grad_gates - jnp.sum(grad_gates * gates, axis=-1, keepdims=True))
         ).astype(BF16)
         GR[0:NE] = GR[0:NE] + tn(grad_logits, N2[m])[0:NE]
-        grad = nn(PM[m, 0] + PM[m, 1], RET[m, 1].reshape(S, D)) + nt(grad_logits, small)
+        grad = nn(PM[m, 0] + PM[m, 1], DXB[m].reshape(S, D)) + nt(grad_logits, small)
         hat, rstd = normalize(MID[m])
         GR[NE + 1 : NE + 2] = GR[NE + 1 : NE + 2] + jnp.sum(grad * hat, axis=0, keepdims=True)
         grad_middle = upstream + normalize_back(grad * gain_two, hat, rstd)
@@ -803,12 +854,16 @@
         full = GM[m] + normalize_back(grad * gain_one, hat, rstd)
         b["IG"][m, :, 0, :] = full[0:T]
 
-    sums_next(1)
+    sums_now((1, 0), (1, 1))
     for m in range(M):
-        exchanged(RET, m, s_back[m])
+        exchanged(DXB, m, s_dx[m])
+        exchanged(GCB, m, s_gc[m])
+        if m == M - 1:
+            for k in range(M):
+                exchange(YS, YB, k, s_y[k])
         backward_top(m)
         backward_heads(m)
-        sums_next(2)
+        sums_now(*(((2, 0),) if m == 0 else ((1, 2), (2, 1)) if m == 1 else ()))
     for k in range(nb):
         part = tn(
             ATT[...].reshape(M * TP, D), N2[:, :, k * TW : (k + 1) * TW].reshape(M * TP, TW)
@@ -829,8 +884,6 @@
     sent_later(s_r1, RB1)
     for m in range(M):
         backward_end(m)
-    b["AO"][...] = b["AR"][...].astype(BF16)
-    kept.append(fetch(b["AO"], act))
     kept.append(fetch(b["IG"], igrad))
     GB[...] = GR[...].astype(BF16)
     r_b1 = one_send(GB, SB1, sibling)
@@ -853,7 +906,7 @@
     for d in range(1, G):
         send(SB2.at[y], SB2.at[y], s_b2 + d, r_b2 + d, at(z, x, ((y + d) % G) * 2 + core))
         sent_later(s_b2 + d, SB2.at[y])
-    sums_next(1)
+    sums_now((2, 2), (1, 3))
     for d in range(1, G):
         q = (y + G - d) % G
         arrived(RY1.at[q], r_ry1 + d)
@@ -875,7 +928,6 @@
         total = total + SB2[j].astype(F32)
     SB3[x] = total.astype(BF16)
     r_b3 = one_send(SB3.at[x], SB3.at[x], across)
-    sums_next(1)
     arrived(RX2, r_rx2)
     DG[e, 0:h, x] = DG[e, 0:h, x] + RX2[...]
     for d in range(1, G):
@@ -894,9 +946,16 @@
         send(SB4.at[z], SB4.at[z], s_b4, r_b4, at((z + dz) % nz, x, e))
     sent_later(s_b4, SB4.at[0 : nz - 1])
     sums_rest()
-    ends = [0, nz - 1] + list(range(1, nz - 1))
-    for k in ends[:2]:
+    for k in (0, nz - 1):
         sums_end_in(k)
+    sums_end_out()
+    for k in range(1, nz - 1):
+        sums_end_in(k)
+    for m in range(M):
+        exchanged(YB, m, s_y[m])
+        outputs(m)
+    b["AO"][...] = b["AR"][...].astype(BF16)
+    kept.append(fetch(b["AO"], act))
     RZ[z] = DG[e, z, x]
     arrived(RZ.at[0 : nz - 1], r_rz)
     total = RZ[0].astype(F32)
@@ -929,9 +988,6 @@
     kept.append(fetch(b["GS"].at[0:NE], grouter))
     kept.append(fetch(b["GS"].at[NE : NE + 1], ggain1))
     kept.append(fetch(b["GS"].at[NE + 1 : NE + 2], ggain2))
-    sums_end_out()
-    for k in ends[2:]:
-        sums_end_in(k)
     sums_close()
     arrived(FIN.at[0 : E - 1], r_fe)
     for k in range(nq):
@@ -983,7 +1039,7 @@
     scratch = scratch_of(c)
     names = list(scratch)
     nz, G = c["nz"], c["G"]
-    counts = (31 + 6 * G, 14 + 16 * nz + 2 * nz * nz + G * nz + 5 * G, 20)
+    counts = (39 + 6 * G, 22 + 16 * nz + 2 * nz * nz + G * nz + 5 * G, 20)
     shapes = (
         ((rows, micro, width), BF16),
         ((micro, rows, 1, width), F32),

time: 158 us -> 143 us (0.905)
  Pallas kernels: 157 us -> 142 us
    pallas_call x1, Pallas kernels: 154 us -> 139 us  [body(): pl.pallas_call(functools.partial(kernel, c, names, counts), out_shape=sha...]
where the time goes in v3:
time: 143 us
  Pallas kernels  142 us (99%)
    pallas_call x1, Pallas kernels, body(): pl.pallas_call(functools.partial(kernel, c, names, counts), out_shape=sha...  139 us
    pallas_call x1, Pallas kernels, body(): pl.pallas_call(hand_over, out_shape=shapes, in_specs=[anywhere] * 9, out_...  3.27 us

profile of v3, /device:TPU:0, one launch (start us, length us, event | category | flops | bytes accessed | tf_op | source)
XLA Modules:
  0.0 142.8 jit_solution(16151172259338773774)
XLA Ops:
  0.6 138.7 %shard_map.169 = (bf16[197,2,512]{2,1,0:T(2,128)(2,1)}, f32[2,197,1,512]{3,2,1,0:T(1,128)}, f32[64,1536]{1,0:T(8,128)}, f32[64,512]{1,0:T(8,128)}, f32[1,64]{1,0...) custom-call(bf16[197,2,512]{2,1,0:T(2,128)(2,1)} %bitcast.21, ...), custom_call_target="tpu_custom_call" | custom-call | tf_op jit(solution)/shard_map/pallas_call | solution.py:1056
  139.3 3.3 %shard_map.170 = (bf16[197,2,512]{2,1,0:T(2,128)(2,1)}, f32[2,197,1,512]{3,2,1,0:T(1,128)}, f32[64,1536]{1,0:T(8,128)}, f32[64,512]{1,0:T(8,128)}, f32[1,64]{1,0...) custom-call(bf16[197,2,512]{2,1,0:T(2,128)(2,1)} %get-tuple-element.27.refs_0_, ...), custom_call_target="tpu_custom_call" | custom-call | tf_op jit(solution)/shard_map/pallas_call | solution.py:1078
